TPU v7x, 256 devices: a whole 4x4x8 slice. The times are simulated.
256 devices in a mesh: band: 8 (over y, core), fft: 32 (over x, z).
Axes of the slice: x: 4, y: 4, z: 8, core: 2. Of those that a mesh axis runs over, the one named last changes fastest.
Arguments:
- psi: bfloat16 [16, 2, 2560, 128], P('band', None, 'fft'), may hold values from -6 to 6
- stick_col: int32 [2560], replicated, may hold values from 0 to 15420, as said below
- stick_len: int32 [2560], replicated, may hold values from 0 to 121, as said below
- plane_z: int32 [256], replicated, may hold values from -1 to 239, as said below
- potential: float32 [256, 57600], P('fft'), may hold values from -12 to 12
- beta: bfloat16 [8, 8, 2, 2560, 128], P('band', None, None, 'fft'), may hold values from -0.01953125 to 0.01953125
- coupling: float32 [8, 8, 8], replicated, may hold values from -80 to 80
Outputs:
- hpsi: float32 [16, 2, 2560, 128], P('band', None, 'fft')
Inputs may be any that keep to these rules, and one draw needn't show every extreme that they name: stick_col[i] = (gx + 60) * 128 + gy + 60 for the stick in slot i, where slots i = d * 80 .. (d + 1) * 80 - 1 belong to index d of fft and the used ones come first; every used stick has gx^2 + gy^2 <= 60^2 and no column is used twice; empty slots hold 0. stick_len[i] = 2 h + 1 with h the largest integer such that gx^2 + gy^2 + h^2 <= 60^2, for used slots, and 0 for empty ones; an index of fft holds at most 80 sticks, one holds exactly 80, and all together hold 1280. Slot t of index d of fft is plane_z[d * 8 + t], or -1 when empty; used slots come first and hold consecutive planes, every plane 0 .. 239 is held once, and the numbers of planes held by two indices differ by at most one.
All inputs are finite; a program needn't handle non-finite values.
Results may differ from a plain program's by a relative error of at most 0.015.
Values may be sent and summed in bfloat16 or wider, within the bound.
A program may use at most 64 MiB of HBM per device.

v0:
```python
import functools
import math

import jax
import jax.numpy as jnp
import numpy as np
from jax import lax
from jax.experimental import pallas as pl
from jax.experimental.pallas import tpu as pltpu
from jax.sharding import PartitionSpec as P

NG = 240
RAD = 60
W = 128
SLOTS = 80
PLANES = 8
LOW = 16
F32 = jnp.float32
BF16 = jnp.bfloat16
MESH = pl.DeviceIdType.MESH


def tables():
    wave = np.arange(W) - RAD
    pos = np.arange(256)
    angle = 2.0 * np.pi * ((wave[:, None] * pos[None, :]) % NG) / NG
    inside = (pos < NG)[None, :]
    co, si = np.cos(angle) * inside, np.sin(angle) * inside
    z_re = np.concatenate([co.T, -si.T], axis=1)
    z_im = np.concatenate([si.T, co.T], axis=1)
    y_out = np.block([[co, si], [-si, co]])
    y_back = y_out.T
    cx, sx = co[:, :NG].T, si[:, :NG].T
    x_out = np.block([[cx, -sx], [sx, cx]])
    x_back = x_out.T
    return [np.asarray(t, np.float32).astype(jnp.bfloat16) for t in (np.stack([z_re, z_im]), y_out, x_out, x_back, y_back)]


def iota(shape, dim):
    return lax.broadcasted_iota(jnp.int32, shape, dim)


def dot(a, b, dims=((1,), (0,)), precision=None):
    return lax.dot_general(a, b, (dims, ((), ())), preferred_element_type=F32, precision=precision)


NT = ((1,), (1,))
TN = ((0,), (0,))


def kernel(
    n_band, n_fft,
    len_s, col_s, plane_ref, col_ref, psi_ref, pot_ref, beta_ref, coup_ref,
    zt_ref, yf_ref, xf_ref, xb_ref, yb_ref,
    out_ref,
    lenb, colb, psi2, z_tab, send1, recv1, send2, recv2,
    xhot, yhot, v3, dense, lhs, yin, boxb,
    gath, beta_f, beta_t, psi_f, psi_t, part_send, part_recv, term_f, term_send, term_recv,
    s1, r1, s2, r2, sg, rg, sp, rp, sn, rn,
):
    f = lax.axis_index("fft")
    g = lax.axis_index("band")
    nb = 2
    tot = n_fft * SLOTS
    nq = 2 * PLANES
    groups = n_fft // 8

    barrier = pltpu.get_barrier_semaphore()

    @pl.loop(1, n_fft)
    def _(k):
        pl.semaphore_signal(barrier, inc=1, device_id={"fft": lax.rem(f + k, n_fft)}, device_id_type=MESH)

    @pl.loop(1, n_band)
    def _(k):
        pl.semaphore_signal(barrier, inc=1, device_id={"band": lax.rem(g + k, n_band)}, device_id_type=MESH)

    @pl.loop(0, SLOTS)
    def _(s):
        lenb[pl.ds(s, 1), :] = jnp.full((1, W), len_s[f * SLOTS + s], jnp.int32)
        colb[pl.ds(s, 1), :] = jnp.full((1, W), col_s[f * SLOTS + s], jnp.int32)

    wave_z = iota((SLOTS, W), 1) - RAD
    in_sphere = (2 * jnp.abs(wave_z) < lenb[...]).astype(F32)
    psi2[...] = jnp.zeros(psi2.shape, BF16)
    for b in range(nb):
        for c in range(2):
            psi2[b, 0:SLOTS, c * W:(c + 1) * W] = (psi_ref[b, c].astype(F32) * in_sphere).astype(BF16)

    n_slot = n_fft * PLANES
    hot_z = (iota((256, n_slot), 0) == plane_ref[...]).astype(F32).T.astype(BF16)
    z_re = dot(hot_z, zt_ref[0]).reshape(n_fft, 1, PLANES, 256)
    z_im = dot(hot_z, zt_ref[1]).reshape(n_fft, 1, PLANES, 256)
    z_tab[...] = jnp.concatenate([z_re, z_im], axis=1).reshape(n_fft * nq, 256).astype(BF16)
    for b in range(nb):
        along = dot(z_tab[...], psi2[b], NT)
        send1[b] = along.reshape(n_fft, nq, W).astype(BF16)
        recv1[b, f] = send1[b, f]

    pl.semaphore_wait(barrier, n_fft + n_band - 2)

    def exchange(send, recv, send_sem, recv_sem, b):
        @pl.loop(1, n_fft)
        def _(k):
            e = lax.rem(f + k, n_fft)
            pltpu.make_async_remote_copy(
                src_ref=send.at[b, e], dst_ref=recv.at[b, f], send_sem=send_sem.at[b], recv_sem=recv_sem.at[b],
                device_id={"fft": e}, device_id_type=MESH,
            ).start()

    def wait_bytes(ref, sem):
        pltpu.make_async_copy(ref, ref, sem).wait()

    exchange(send1, recv1, s1, r1, 0)

    @pl.loop(1, n_band)
    def _(k):
        pltpu.make_async_remote_copy(
            src_ref=psi_ref, dst_ref=gath.at[g], send_sem=sg, recv_sem=rg,
            device_id={"band": lax.rem(g + k, n_band)}, device_id_type=MESH,
        ).start()

    exchange(send1, recv1, s1, r1, 1)
    gath[g] = psi_ref[...]

    for r in range(tot // W):
        col = col_ref[r:r + 1, :]
        c, d = col // W, col % W
        low, high = c % LOW, (c // LOW) * W + d
        xhot[:, r * W:(r + 1) * W] = (iota((LOW, W), 0) == low).astype(F32).astype(BF16)
        for m in range(2):
            yhot[m * 512:(m + 1) * 512, r * W:(r + 1) * W] = (iota((512, W), 0) + m * 512 == high).astype(F32).astype(BF16)

    @pl.loop(0, NG // 8)
    def _(m):
        for r in range(8):
            start = 240 * r
            low = start // W * W
            width = 256 if start - low <= 16 else 384
            piece = pot_ref[:, pl.ds(pl.multiple_of(m * 1920 + low, W), width)]
            if start - low:
                piece = pltpu.roll(piece, width - (start - low), 1)
            for c in range(2):
                v3[c, pl.ds(pl.multiple_of((m * 8 + r) * 8, 8), 8), :] = piece[:, c * W:(c + 1) * W]

    for k in range(8):
        for c in range(2):
            beta_f[pl.ds((k * 2 + c) * SLOTS, SLOTS), :] = beta_ref[0, k, c].astype(F32) * in_sphere

    @pl.loop(0, SLOTS)
    def _(s):
        rows = [beta_f[pl.ds(c * SLOTS + s, 8, stride=2 * SLOTS), :] for c in range(2)]
        beta_t[:, pl.ds(pl.multiple_of(s * W, W), W)] = jnp.concatenate(rows, axis=0).astype(BF16)

    spread = (iota((nq * LOW, nq), 0) // LOW == iota((nq * LOW, nq), 1)).astype(F32).astype(BF16)
    gather = (iota((nq, nq * LOW), 1) // LOW == iota((nq, nq * LOW), 0)).astype(F32).astype(BF16)
    lane16 = iota((nq, W), 1)

    def to_planes(b):
        wait_bytes(recv1.at[b, pl.ds(0, n_fft - 1)], r1.at[b])

        @pl.loop(0, groups)
        def _(h):
            outs = [jnp.zeros((nq, W), F32)] * 5
            for i in range(8):
                piece = recv1[b, h * 8 + i].astype(F32)
                off = 80 * i % W
                first = 80 * i // W
                rolled = pltpu.roll(piece, off, 1) if off else piece
                top = min(off + 80, W)
                outs[first] = jnp.where((lane16 >= off) & (lane16 < top), rolled, outs[first])
                if off + 80 > W:
                    outs[first + 1] = jnp.where(lane16 < off + 80 - W, rolled, outs[first + 1])
            at = pl.ds(pl.multiple_of(h * 640, W), 640)
            piece = jnp.concatenate(outs, axis=1).astype(BF16)
            dense[:, at] = piece
            repeated = dot(spread, piece).astype(BF16).reshape(nq, LOW, 640)
            lhs[:, at] = (repeated * xhot[:, at][None]).reshape(nq * LOW, 640)

        @pl.loop(0, 4)
        def _(n):
            placed = dot(lhs[...], yhot[pl.ds(pl.multiple_of(n * 256, 256), 256), :], NT).astype(BF16)
            placed = placed.reshape(2, PLANES, LOW, 256)
            for h in range(2):
                for c in range(2):
                    yin[:, pl.ds(pl.multiple_of((n * 2 + h) * LOW, LOW), LOW), c * W:(c + 1) * W] = placed[c, :, :, h * W:(h + 1) * W]

        @pl.loop(0, PLANES // 2)
        def _(pair):
            for u in range(2):
                t = pair * 2 + u
                half = dot(yin[t], yf_ref[...]).astype(BF16)
                half = jnp.concatenate([half[:, :256], half[:, 256:]], axis=0)
                full = dot(xf_ref[...], half).reshape(2, NG, 256)
                weight = jnp.concatenate([v3[c, pl.ds(t, NG, stride=PLANES), :] for c in range(2)], axis=1)
                weighted = (full * weight[None]).astype(BF16).reshape(2 * NG, 256)
                back = dot(xb_ref[...], weighted).astype(BF16)
                back = jnp.concatenate([back[:W], back[W:]], axis=1)
                box = dot(back, yb_ref[...]).astype(BF16)
                for c in range(2):
                    for h in range(W // LOW):
                        boxb[c, t, :, h * W:(h + 1) * W] = box[h * LOW:(h + 1) * LOW, c * W:(c + 1) * W]

    def to_sticks(b):
        boxes = boxb[...].reshape(nq * LOW, 1024)

        @pl.loop(0, tot // 640)
        def _(h):
            at = pl.ds(pl.multiple_of(h * 640, W), 640)
            rows = dot(boxes, yhot[:, at]).astype(BF16).reshape(nq, LOW, 640) * xhot[:, at][None]
            picked = dot(gather, rows.reshape(nq * LOW, 640))
            for i in range(8):
                off = 80 * i % W
                first = 80 * i // W
                piece = picked[:, first * W:(first + 1) * W]
                if off:
                    piece = pltpu.roll(piece, W - off, 1)
                if off + 80 > W:
                    other = pltpu.roll(picked[:, (first + 1) * W:(first + 2) * W], W - off, 1)
                    piece = jnp.where(lane16 < W - off, piece, other)
                send2[b, h * 8 + i] = jnp.where(lane16 < 80, piece, 0.0).astype(BF16)

        recv2[b, f] = send2[b, f]
        exchange(send2, recv2, s2, r2, b)

    nbr = 2 * nb * n_band
    swap = (
        ((iota((nbr, nbr), 0) == iota((nbr, nbr), 1) + 1) & (iota((nbr, nbr), 0) % 2 == 1)).astype(F32)
        - ((iota((nbr, nbr), 0) + 1 == iota((nbr, nbr), 1)) & (iota((nbr, nbr), 0) % 2 == 0)).astype(F32)
    )

    def project():
        wait_bytes(gath.at[pl.ds(0, n_band - 1)], rg)
        for h in range(n_band):
            psi_f[pl.ds(h * 4 * SLOTS, 4 * SLOTS), :] = gath[h].reshape(4 * SLOTS, W).astype(F32)

        @pl.loop(0, SLOTS)
        def _(s):
            psi_t[:, pl.ds(pl.multiple_of(s * W, W), W)] = psi_f[pl.ds(s, nbr, stride=SLOTS), :].astype(BF16)

        prod = dot(beta_t[...], psi_t[...], NT)
        part = prod[:8] + dot(prod[8:], swap, precision=lax.Precision.HIGHEST)
        part_send[...] = jnp.zeros((8, W), F32)
        part_send[:, :nbr] = part
        part_recv[f] = part_send[...]

        @pl.loop(1, n_fft)
        def _(k):
            pltpu.make_async_remote_copy(
                src_ref=part_send, dst_ref=part_recv.at[f], send_sem=sp, recv_sem=rp,
                device_id={"fft": lax.rem(f + k, n_fft)}, device_id_type=MESH,
            ).start()

    def expand():
        wait_bytes(part_recv.at[pl.ds(0, n_fft - 1)], rp)
        whole = jnp.sum(part_recv[...], axis=0)[:, :nbr]
        coeffs = dot(coup_ref[g], whole, precision=lax.Precision.HIGHEST).astype(BF16).astype(F32)
        crossed = dot(coeffs, swap, precision=lax.Precision.HIGHEST)
        factors = jnp.concatenate([coeffs, -crossed], axis=0).astype(BF16)

        @pl.loop(0, SLOTS // 8)
        def _(m):
            terms = dot(factors, beta_t[:, pl.ds(pl.multiple_of(m * 1024, 1024), 1024)], TN)
            for i in range(8):
                term_f[pl.ds(m * 8 + i, nbr, stride=SLOTS), :] = terms[:, i * W:(i + 1) * W]

        for h in range(n_band):
            term_send[h] = term_f[pl.ds(h * 4 * SLOTS, 4 * SLOTS), :].astype(BF16)
        term_recv[g] = term_send[g]

        @pl.loop(1, n_band)
        def _(k):
            e = lax.rem(g + k, n_band)
            pltpu.make_async_remote_copy(
                src_ref=term_send.at[e], dst_ref=term_recv.at[g], send_sem=sn, recv_sem=rn,
                device_id={"band": e}, device_id_type=MESH,
            ).start()

    to_planes(0)
    project()
    to_sticks(0)
    to_planes(1)
    expand()
    to_sticks(1)

    gx, gy = colb[...] // W - RAD, colb[...] % W - RAD
    kinetic = (gx * gx + gy * gy + wave_z * wave_z).astype(F32) / float(RAD * RAD)
    wait_bytes(term_recv.at[pl.ds(0, n_band - 1)], rn)
    for b in range(nb):
        wait_bytes(recv2.at[b, pl.ds(0, n_fft - 1)], r2.at[b])
        local = dot(recv2[b].reshape(n_fft * nq, W), z_tab[...], TN) * (1.0 / float(NG**3))
        for c in range(2):
            at = pl.ds((b * 2 + c) * SLOTS, SLOTS)
            nonlocal_sum = term_recv[0, at, :].astype(F32)
            for h in range(1, n_band):
                nonlocal_sum = nonlocal_sum + term_recv[h, at, :].astype(F32)
            wave = psi_ref[b, c].astype(F32) * in_sphere
            out_ref[b, c] = in_sphere * (kinetic * wave + local[:SLOTS, c * W:(c + 1) * W] + nonlocal_sum)

    for b in range(nb):
        wait_bytes(send1.at[b, pl.ds(0, n_fft - 1)], s1.at[b])
        wait_bytes(send2.at[b, pl.ds(0, n_fft - 1)], s2.at[b])
    wait_bytes(gath.at[pl.ds(0, n_band - 1)], sg)
    wait_bytes(part_recv.at[pl.ds(0, n_fft - 1)], sp)
    wait_bytes(term_send.at[pl.ds(0, n_band - 1)], sn)


def body(n_band, n_fft, psi, stick_col, stick_len, plane_z, potential, beta, coupling):
    tot = n_fft * SLOTS
    n_slot = n_fft * PLANES
    nq = 2 * PLANES
    nbr = 4 * n_band
    consts = [jnp.asarray(t) for t in tables()]
    vmem = pl.BlockSpec(memory_space=pltpu.VMEM)
    smem = pl.BlockSpec(memory_space=pltpu.SMEM)
    dma = pltpu.SemaphoreType.DMA
    return pl.pallas_call(
        functools.partial(kernel, n_band, n_fft),
        out_shape=jax.ShapeDtypeStruct(psi.shape, F32),
        in_specs=[smem, smem] + [vmem] * 11,
        out_specs=vmem,
        scratch_shapes=[
            pltpu.VMEM((SLOTS, W), jnp.int32),
            pltpu.VMEM((SLOTS, W), jnp.int32),
            pltpu.VMEM((2, W, 2 * W), BF16),
            pltpu.VMEM((n_fft * nq, 2 * W), BF16),
            pltpu.VMEM((2, n_fft, nq, W), BF16),
            pltpu.VMEM((2, n_fft, nq, W), BF16),
            pltpu.VMEM((2, n_fft, nq, W), BF16),
            pltpu.VMEM((2, n_fft, nq, W), BF16),
            pltpu.VMEM((LOW, tot), BF16),
            pltpu.VMEM((1024, tot), BF16),
            pltpu.VMEM((2, NG * PLANES, W), F32),
            pltpu.VMEM((nq, tot), BF16),
            pltpu.VMEM((nq * LOW, tot), BF16),
            pltpu.VMEM((PLANES, W, 2 * W), BF16),
            pltpu.VMEM((2, PLANES, LOW, 1024), BF16),
            pltpu.VMEM((n_band, 2, 2, SLOTS, W), BF16),
            pltpu.VMEM((16 * SLOTS, W), F32),
            pltpu.VMEM((16, SLOTS * W), BF16),
            pltpu.VMEM((nbr * SLOTS, W), F32),
            pltpu.VMEM((nbr, SLOTS * W), BF16),
            pltpu.VMEM((8, W), F32),
            pltpu.VMEM((n_fft, 8, W), F32),
            pltpu.VMEM((nbr * SLOTS, W), F32),
            pltpu.VMEM((n_band, 4 * SLOTS, W), BF16),
            pltpu.VMEM((n_band, 4 * SLOTS, W), BF16),
            dma((2,)), dma((2,)), dma((2,)), dma((2,)),
            dma, dma, dma, dma, dma, dma,
        ],
        compiler_params=pltpu.CompilerParams(
            collective_id=0, has_side_effects=True, vmem_limit_bytes=56 * 1024 * 1024
        ),
    )(
        stick_len, stick_col, plane_z.reshape(1, n_slot), stick_col.reshape(tot // W, W),
        psi, potential, beta, coupling, *consts,
    )


def solution(mesh):
    in_specs = (
        P("band", None, "fft", None),
        P(),
        P(),
        P(),
        P("fft", None),
        P("band", None, None, "fft", None),
        P(),
    )
    out_specs = P("band", None, "fft", None)
    part = functools.partial(body, mesh.shape["band"], mesh.shape["fft"])
    return jax.shard_map(part, mesh=mesh, in_specs=in_specs, out_specs=out_specs, check_vma=False)
```

profile of v0, /device:TPU:16, one launch (start us, length us, event | category | flops | bytes accessed | tf_op | source)
XLA Modules:
  0.0 56.7 jit_solution(1644388795712995303)
XLA Ops:
  0.0 55.1 %shard_map.118 = f32[2,2,80,128]{3,2,1,0:T(8,128)} custom-call(s32[2560]{0:T(1024)} %len_s.1, s32[2560]{0:T(1024)} %col_s.1, s32[1,256]{1,0:T(1,128)} %bitcast.3, s32[20,128]{1,0:T(8,128)} %bitcast.2, bf16[2,2,80,128]{3,2,1,0:T(8,128)(2,1)} %psi_ref.1, f32[8,57600]{1,0:T(8,128)} %pot_ref.1, bf16[1,8,2,80,128]{4,3,2,1,0:T(8,128)(2,1)} %beta_ref.1, ...), custom_call_target="tpu_custom_call" | custom-call | tf_op jit(solution)/shard_map/pallas_call | solution.py:317
  55.1 1.6 %copy.14 = f32[2,2,80,128]{3,2,1,0:T(8,128)} copy(f32[2,2,80,128]{3,2,1,0:T(8,128)} %shard_map.118) | data formatting | bytes 327680
where the time goes:
time: 57.4 us; the launch traced here: 56.7 us
  Pallas kernels  55.1 us (96%)
  local copies, waits for them, and re-layouts  1.59 us (3%)
    pallas_call x1, Pallas kernels, body(): pl.pallas_call(functools.partial(kernel, n_band, n_fft), out_shape=jax.Sh...  55.1 us
    unnamed x1, local copies, waits for them, and re-layouts  1.59 us

commit v1 on v0

--- a/solution.py
+++ b/solution.py
@@ -14,7 +14,8 @@
 W = 128
 SLOTS = 80
 PLANES = 8
-LOW = 16
+LOW = 64
+PAD = 88
 F32 = jnp.float32
 BF16 = jnp.bfloat16
 MESH = pl.DeviceIdType.MESH
@@ -32,6 +33,7 @@
     y_back = y_out.T
     cx, sx = co[:, :NG].T, si[:, :NG].T
     x_out = np.block([[cx, -sx], [sx, cx]])
+    x_out = x_out.reshape(2 * NG, 2, W).transpose(0, 2, 1).reshape(2 * NG, 2 * W)
     x_back = x_out.T
     return [np.asarray(t, np.float32).astype(jnp.bfloat16) for t in (np.stack([z_re, z_im]), y_out, x_out, x_back, y_back)]
 
@@ -54,7 +56,7 @@
     zt_ref, yf_ref, xf_ref, xb_ref, yb_ref,
     out_ref,
     lenb, colb, psi2, z_tab, send1, recv1, send2, recv2,
-    xhot, yhot, v3, dense, lhs, yin, boxb,
+    chi_f, chi_b, yhot, v3, dense, box, boxes, picked,
     gath, beta_f, beta_t, psi_f, psi_t, part_send, part_recv, term_f, term_send, term_recv,
     s1, r1, s2, r2, sg, rg, sp, rp, sn, rn,
 ):
@@ -123,42 +125,48 @@
     exchange(send1, recv1, s1, r1, 1)
     gath[g] = psi_ref[...]
 
-    for r in range(tot // W):
-        col = col_ref[r:r + 1, :]
-        c, d = col // W, col % W
-        low, high = c % LOW, (c // LOW) * W + d
-        xhot[:, r * W:(r + 1) * W] = (iota((LOW, W), 0) == low).astype(F32).astype(BF16)
-        for m in range(2):
-            yhot[m * 512:(m + 1) * 512, r * W:(r + 1) * W] = (iota((512, W), 0) + m * 512 == high).astype(F32).astype(BF16)
-
-    @pl.loop(0, NG // 8)
-    def _(m):
-        for r in range(8):
-            start = 240 * r
-            low = start // W * W
-            width = 256 if start - low <= 16 else 384
-            piece = pot_ref[:, pl.ds(pl.multiple_of(m * 1920 + low, W), width)]
-            if start - low:
-                piece = pltpu.roll(piece, width - (start - low), 1)
+    def place_tables():
+        for r in range(tot // W):
+            col = col_ref[r:r + 1, :]
+            c, d = col // W, col % W
+            low = jnp.broadcast_to(c % LOW, (nq, W)).astype(F32)
+            chi_f[:, r * W:(r + 1) * W] = low[:8]
+            chi_b[:, r * W:(r + 1) * W] = low.astype(BF16)
+            yhot[:, r * W:(r + 1) * W] = (iota((2 * W, W), 0) == (c // LOW) * W + d).astype(F32).astype(BF16)
+
+    def potential_rows():
+        @pl.loop(0, NG // 24)
+        def _(m3):
+            for u in range(3):
+                m = m3 * 3 + u
+                for r in range(8):
+                    start = 240 * r
+                    low = start // W * W
+                    width = 256 if start - low <= 16 else 384
+                    piece = pot_ref[:, pl.ds(pl.multiple_of(m * 1920 + low, W), width)]
+                    if start - low:
+                        piece = pltpu.roll(piece, width - (start - low), 1)
+                    for c in range(2):
+                        v3[c, pl.ds(pl.multiple_of((m * 8 + r) * 8, 8), 8), :] = piece[:, c * W:(c + 1) * W]
+
+    def projector_rows():
+        for k in range(8):
             for c in range(2):
-                v3[c, pl.ds(pl.multiple_of((m * 8 + r) * 8, 8), 8), :] = piece[:, c * W:(c + 1) * W]
-
-    for k in range(8):
-        for c in range(2):
-            beta_f[pl.ds((k * 2 + c) * SLOTS, SLOTS), :] = beta_ref[0, k, c].astype(F32) * in_sphere
-
-    @pl.loop(0, SLOTS)
-    def _(s):
-        rows = [beta_f[pl.ds(c * SLOTS + s, 8, stride=2 * SLOTS), :] for c in range(2)]
-        beta_t[:, pl.ds(pl.multiple_of(s * W, W), W)] = jnp.concatenate(rows, axis=0).astype(BF16)
-
-    spread = (iota((nq * LOW, nq), 0) // LOW == iota((nq * LOW, nq), 1)).astype(F32).astype(BF16)
-    gather = (iota((nq, nq * LOW), 1) // LOW == iota((nq, nq * LOW), 0)).astype(F32).astype(BF16)
+                beta_f[pl.ds((c * 8 + k) * PAD, SLOTS), :] = beta_ref[0, k, c].astype(F32) * in_sphere
+
+        @pl.loop(0, SLOTS // 4)
+        def _(s4):
+            for u in range(4):
+                s = s4 * 4 + u
+                rows = beta_f[pl.ds(s, 16, stride=PAD), :]
+                beta_t[:, pl.ds(pl.multiple_of(s * W, W), W)] = rows.astype(BF16)
+
     lane16 = iota((nq, W), 1)
 
     def to_planes(b):
         wait_bytes(recv1.at[b, pl.ds(0, n_fft - 1)], r1.at[b])
 
+    def spread_sticks(b):
         @pl.loop(0, groups)
         def _(h):
             outs = [jnp.zeros((nq, W), F32)] * 5
@@ -172,51 +180,75 @@
                 if off + 80 > W:
                     outs[first + 1] = jnp.where(lane16 < off + 80 - W, rolled, outs[first + 1])
             at = pl.ds(pl.multiple_of(h * 640, W), 640)
-            piece = jnp.concatenate(outs, axis=1).astype(BF16)
-            dense[:, at] = piece
-            repeated = dot(spread, piece).astype(BF16).reshape(nq, LOW, 640)
-            lhs[:, at] = (repeated * xhot[:, at][None]).reshape(nq * LOW, 640)
-
-        @pl.loop(0, 4)
-        def _(n):
-            placed = dot(lhs[...], yhot[pl.ds(pl.multiple_of(n * 256, 256), 256), :], NT).astype(BF16)
-            placed = placed.reshape(2, PLANES, LOW, 256)
+            dense[:, at] = jnp.concatenate(outs, axis=1).astype(BF16)
+
+    def place_columns(b):
+        @pl.loop(0, 2)
+        def _(m):
+            first = (m * (LOW // 2)).astype(F32).astype(BF16)
+            sticks = dense[...]
+            place = chi_b[...] - first
+            rows = [jnp.where(place == jnp.asarray(i, BF16), sticks, jnp.asarray(0, BF16)) for i in range(LOW // 2)]
+            placed = dot(jnp.concatenate(rows, axis=0), yhot[...], NT)
+            at = pl.ds(pl.multiple_of(m * (LOW // 2 * nq), LOW // 2 * nq), LOW // 2 * nq)
             for h in range(2):
-                for c in range(2):
-                    yin[:, pl.ds(pl.multiple_of((n * 2 + h) * LOW, LOW), LOW), c * W:(c + 1) * W] = placed[c, :, :, h * W:(h + 1) * W]
-
-        @pl.loop(0, PLANES // 2)
-        def _(pair):
-            for u in range(2):
-                t = pair * 2 + u
-                half = dot(yin[t], yf_ref[...]).astype(BF16)
-                half = jnp.concatenate([half[:, :256], half[:, 256:]], axis=0)
-                full = dot(xf_ref[...], half).reshape(2, NG, 256)
-                weight = jnp.concatenate([v3[c, pl.ds(t, NG, stride=PLANES), :] for c in range(2)], axis=1)
-                weighted = (full * weight[None]).astype(BF16).reshape(2 * NG, 256)
-                back = dot(xb_ref[...], weighted).astype(BF16)
-                back = jnp.concatenate([back[:W], back[W:]], axis=1)
-                box = dot(back, yb_ref[...]).astype(BF16)
-                for c in range(2):
-                    for h in range(W // LOW):
-                        boxb[c, t, :, h * W:(h + 1) * W] = box[h * LOW:(h + 1) * LOW, c * W:(c + 1) * W]
+                box[h, at, :] = placed[:, h * W:(h + 1) * W]
+
+    def transform():
+        @pl.loop(0, PLANES // 4)
+        def _(quad):
+            along_x = []
+            for p in range(2):
+                pair = []
+                for u in range(2):
+                    t = quad * 4 + p * 2 + u
+                    pair.append(jnp.concatenate([box[h, pl.ds(t, W, stride=PLANES), :] for h in range(2)], axis=0))
+                wide = dot(xf_ref[...], jnp.concatenate(pair, axis=1).astype(BF16)).astype(BF16)
+                for u in range(2):
+                    part = wide[:, u * W:(u + 1) * W]
+                    along_x.append(jnp.concatenate([part[:NG], part[NG:]], axis=1))
+            full = dot(jnp.concatenate(along_x, axis=0), yf_ref[...])
+            weighted = []
+            for u in range(4):
+                weight = [v3[c, pl.ds(quad * 4 + u, NG, stride=PLANES), :] for c in range(2)]
+                weighted.append((full[u * NG:(u + 1) * NG] * jnp.concatenate(weight * 2, axis=1)).astype(BF16))
+            back = dot(jnp.concatenate(weighted, axis=0), yb_ref[...]).astype(BF16)
+            for p in range(2):
+                pair = [back[(p * 2 + u) * NG:(p * 2 + u + 1) * NG] for u in range(2)]
+                pair = [jnp.concatenate([part[:, :W], part[:, W:]], axis=0) for part in pair]
+                wide = dot(xb_ref[...], jnp.concatenate(pair, axis=1))
+                for u in range(2):
+                    t = quad * 4 + p * 2 + u
+                    for h in range(2):
+                        box[h, pl.ds(t, W, stride=PLANES), :] = wide[h * W:(h + 1) * W, u * W:(u + 1) * W]
 
     def to_sticks(b):
-        boxes = boxb[...].reshape(nq * LOW, 1024)
-
-        @pl.loop(0, tot // 640)
+        boxes[...] = jnp.concatenate([box[0], box[1]], axis=1).astype(BF16)
+
+        step = 512 if tot % 512 == 0 else 640
+
+        @pl.loop(0, tot // step)
+        def _(h):
+            at = pl.ds(pl.multiple_of(h * step, W), step)
+            rows = dot(boxes[...], yhot[:, at])
+            place = jnp.concatenate([chi_f[:, at]] * 2, axis=0)
+            found = jnp.zeros((nq, step), F32)
+            for i in range(LOW):
+                found = jnp.where(place == float(i), rows[i * nq:(i + 1) * nq], found)
+            picked[:, at] = found
+
+        @pl.loop(0, groups)
         def _(h):
             at = pl.ds(pl.multiple_of(h * 640, W), 640)
-            rows = dot(boxes, yhot[:, at]).astype(BF16).reshape(nq, LOW, 640) * xhot[:, at][None]
-            picked = dot(gather, rows.reshape(nq * LOW, 640))
+            found = picked[:, at]
             for i in range(8):
                 off = 80 * i % W
                 first = 80 * i // W
-                piece = picked[:, first * W:(first + 1) * W]
+                piece = found[:, first * W:(first + 1) * W]
                 if off:
                     piece = pltpu.roll(piece, W - off, 1)
                 if off + 80 > W:
-                    other = pltpu.roll(picked[:, (first + 1) * W:(first + 2) * W], W - off, 1)
+                    other = pltpu.roll(found[:, (first + 1) * W:(first + 2) * W], W - off, 1)
                     piece = jnp.where(lane16 < W - off, piece, other)
                 send2[b, h * 8 + i] = jnp.where(lane16 < 80, piece, 0.0).astype(BF16)
 
@@ -231,12 +263,17 @@
 
     def project():
         wait_bytes(gath.at[pl.ds(0, n_band - 1)], rg)
-        for h in range(n_band):
-            psi_f[pl.ds(h * 4 * SLOTS, 4 * SLOTS), :] = gath[h].reshape(4 * SLOTS, W).astype(F32)
-
-        @pl.loop(0, SLOTS)
-        def _(s):
-            psi_t[:, pl.ds(pl.multiple_of(s * W, W), W)] = psi_f[pl.ds(s, nbr, stride=SLOTS), :].astype(BF16)
+        @pl.loop(0, n_band)
+        def _(h):
+            for b in range(nb):
+                for c in range(2):
+                    psi_f[pl.ds(pl.multiple_of((h * 4 + b * 2 + c) * PAD, 8), SLOTS), :] = gath[h, b, c].astype(F32)
+
+        @pl.loop(0, SLOTS // 4)
+        def _(s4):
+            for u in range(4):
+                s = s4 * 4 + u
+                psi_t[:, pl.ds(pl.multiple_of(s * W, W), W)] = psi_f[pl.ds(s, nbr, stride=PAD), :].astype(BF16)
 
         prod = dot(beta_t[...], psi_t[...], NT)
         part = prod[:8] + dot(prod[8:], swap, precision=lax.Precision.HIGHEST)
@@ -262,10 +299,13 @@
         def _(m):
             terms = dot(factors, beta_t[:, pl.ds(pl.multiple_of(m * 1024, 1024), 1024)], TN)
             for i in range(8):
-                term_f[pl.ds(m * 8 + i, nbr, stride=SLOTS), :] = terms[:, i * W:(i + 1) * W]
-
-        for h in range(n_band):
-            term_send[h] = term_f[pl.ds(h * 4 * SLOTS, 4 * SLOTS), :].astype(BF16)
+                term_f[pl.ds(m * 8 + i, nbr, stride=PAD), :] = terms[:, i * W:(i + 1) * W]
+
+        @pl.loop(0, n_band)
+        def _(h):
+            for i in range(4):
+                term_send[h, i * SLOTS:(i + 1) * SLOTS, :] = term_f[pl.ds(pl.multiple_of((h * 4 + i) * PAD, 8), SLOTS), :].astype(BF16)
+
         term_recv[g] = term_send[g]
 
         @pl.loop(1, n_band)
@@ -276,10 +316,19 @@
                 device_id={"band": e}, device_id_type=MESH,
             ).start()
 
+    place_tables()
+    potential_rows()
+    projector_rows()
     to_planes(0)
+    spread_sticks(0)
+    place_columns(0)
+    transform()
     project()
     to_sticks(0)
     to_planes(1)
+    spread_sticks(1)
+    place_columns(1)
+    transform()
     expand()
     to_sticks(1)
 
@@ -328,21 +377,22 @@
             pltpu.VMEM((2, n_fft, nq, W), BF16),
             pltpu.VMEM((2, n_fft, nq, W), BF16),
             pltpu.VMEM((2, n_fft, nq, W), BF16),
-            pltpu.VMEM((LOW, tot), BF16),
-            pltpu.VMEM((1024, tot), BF16),
+            pltpu.VMEM((8, tot), F32),
+            pltpu.VMEM((nq, tot), BF16),
+            pltpu.VMEM((2 * W, tot), BF16),
             pltpu.VMEM((2, NG * PLANES, W), F32),
             pltpu.VMEM((nq, tot), BF16),
-            pltpu.VMEM((nq * LOW, tot), BF16),
-            pltpu.VMEM((PLANES, W, 2 * W), BF16),
-            pltpu.VMEM((2, PLANES, LOW, 1024), BF16),
+            pltpu.VMEM((2, LOW * nq, W), F32),
+            pltpu.VMEM((LOW * nq, 2 * W), BF16),
+            pltpu.VMEM((nq, tot), F32),
             pltpu.VMEM((n_band, 2, 2, SLOTS, W), BF16),
-            pltpu.VMEM((16 * SLOTS, W), F32),
+            pltpu.VMEM((16 * PAD, W), F32),
             pltpu.VMEM((16, SLOTS * W), BF16),
-            pltpu.VMEM((nbr * SLOTS, W), F32),
+            pltpu.VMEM((nbr * PAD, W), F32),
             pltpu.VMEM((nbr, SLOTS * W), BF16),
             pltpu.VMEM((8, W), F32),
             pltpu.VMEM((n_fft, 8, W), F32),
-            pltpu.VMEM((nbr * SLOTS, W), F32),
+            pltpu.VMEM((nbr * PAD, W), F32),
             pltpu.VMEM((n_band, 4 * SLOTS, W), BF16),
             pltpu.VMEM((n_band, 4 * SLOTS, W), BF16),
             dma((2,)), dma((2,)), dma((2,)), dma((2,)),

time: 57.4 us -> 47.6 us (0.83); the launches traced: 56.7 us -> 47.5 us
  Pallas kernels: 55.1 us -> 45.9 us
    pallas_call x1, Pallas kernels: 55.1 us -> 45.9 us  [body(): pl.pallas_call(functools.partial(kernel, n_band, n_fft), out_shape=jax.Sh...]
where the time goes in v1:
time: 47.6 us; the launch traced here: 47.5 us
  Pallas kernels  45.9 us (96%)
  local copies, waits for them, and re-layouts  1.59 us (3%)
    pallas_call x1, Pallas kernels, body(): pl.pallas_call(functools.partial(kernel, n_band, n_fft), out_shape=jax.Sh...  45.9 us
    unnamed x1, local copies, waits for them, and re-layouts  1.59 us

profile of v1, /device:TPU:16, one launch (start us, length us, event | category | flops | bytes accessed | tf_op | source)
XLA Modules:
  0.0 47.5 jit_solution(12296049703264146110)
XLA Ops:
  0.0 45.9 %shard_map.118 = f32[2,2,80,128]{3,2,1,0:T(8,128)} custom-call(s32[2560]{0:T(1024)} %len_s.1, s32[2560]{0:T(1024)} %col_s.1, s32[1,256]{1,0:T(1,128)} %bitcast.3, s32[20,128]{1,0:T(8,128)} %bitcast.2, bf16[2,2,80,128]{3,2,1,0:T(8,128)(2,1)} %psi_ref.1, f32[8,57600]{1,0:T(8,128)} %pot_ref.1, bf16[1,8,2,80,128]{4,3,2,1,0:T(8,128)(2,1)} %beta_ref.1, ...), custom_call_target="tpu_custom_call" | custom-call | tf_op jit(solution)/shard_map/pallas_call | solution.py:366
  45.9 1.6 %copy.14 = f32[2,2,80,128]{3,2,1,0:T(8,128)} copy(f32[2,2,80,128]{3,2,1,0:T(8,128)} %shard_map.118) | data formatting | bytes 327680

commit v2 on v1

--- a/solution.py
+++ b/solution.py
@@ -52,13 +52,13 @@
 
 def kernel(
     n_band, n_fft,
-    len_s, col_s, plane_ref, col_ref, psi_ref, pot_ref, beta_ref, coup_ref,
-    zt_ref, yf_ref, xf_ref, xb_ref, yb_ref,
-    out_ref,
+    len_h, col_h, plane_h, col2_h, psi_h, pot_h, beta_h, coup_h, zt_h, yf_h, xf_h, xb_h, yb_h,
+    out_h,
+    len_s, col_s, plane_ref, col_ref, psi_ref, pot_ref, beta_ref, coup_ref, zt_ref, yf_ref, xf_ref, xb_ref, yb_ref, out_ref,
     lenb, colb, psi2, z_tab, send1, recv1, send2, recv2,
     chi_f, chi_b, yhot, v3, dense, box, boxes, picked,
-    gath, beta_f, beta_t, psi_f, psi_t, part_send, part_recv, term_f, term_send, term_recv,
-    s1, r1, s2, r2, sg, rg, sp, rp, sn, rn,
+    gath, beta_f, beta_t, psi_f, psi_t, part_send, part_recv, term_f, term_send, term_recv, base,
+    s1, r1, s2, r2, sg, rg, sp, rp, sn, rn, load_sem, out_sem,
 ):
     f = lax.axis_index("fft")
     g = lax.axis_index("band")
@@ -77,7 +77,17 @@
     def _(k):
         pl.semaphore_signal(barrier, inc=1, device_id={"band": lax.rem(g + k, n_band)}, device_id_type=MESH)
 
-    @pl.loop(0, SLOTS)
+    pairs = (
+        (len_h, len_s), (col_h, col_s), (plane_h, plane_ref), (psi_h, psi_ref), (zt_h, zt_ref), (col2_h, col_ref), (pot_h, pot_ref),
+        (beta_h, beta_ref), (xf_h, xf_ref), (yf_h, yf_ref), (yb_h, yb_ref), (xb_h, xb_ref), (coup_h, coup_ref),
+    )
+    loads = [pltpu.make_async_copy(far, near, load_sem.at[i]) for i, (far, near) in enumerate(pairs)]
+    for load in loads:
+        load.start()
+    for load in loads[:5]:
+        load.wait()
+
+    @pl.loop(0, SLOTS, unroll=8)
     def _(s):
         lenb[pl.ds(s, 1), :] = jnp.full((1, W), len_s[f * SLOTS + s], jnp.int32)
         colb[pl.ds(s, 1), :] = jnp.full((1, W), col_s[f * SLOTS + s], jnp.int32)
@@ -133,6 +143,13 @@
             chi_f[:, r * W:(r + 1) * W] = low[:8]
             chi_b[:, r * W:(r + 1) * W] = low.astype(BF16)
             yhot[:, r * W:(r + 1) * W] = (iota((2 * W, W), 0) == (c // LOW) * W + d).astype(F32).astype(BF16)
+
+    def diagonal():
+        gx, gy = colb[...] // W - RAD, colb[...] % W - RAD
+        kinetic = (gx * gx + gy * gy + wave_z * wave_z).astype(F32) / float(RAD * RAD)
+        for b in range(nb):
+            for c in range(2):
+                base[b, c] = kinetic * in_sphere * psi_ref[b, c].astype(F32)
 
     def potential_rows():
         @pl.loop(0, NG // 24)
@@ -225,23 +242,19 @@
     def to_sticks(b):
         boxes[...] = jnp.concatenate([box[0], box[1]], axis=1).astype(BF16)
 
-        step = 512 if tot % 512 == 0 else 640
-
-        @pl.loop(0, tot // step)
-        def _(h):
+        step = 1280 if tot % 1280 == 0 else 640
+        chunks, each = tot // step, step // SLOTS
+
+        @pl.loop(0, chunks)
+        def _(turn):
+            h = lax.rem(turn + f // each, chunks)
             at = pl.ds(pl.multiple_of(h * step, W), step)
             rows = dot(boxes[...], yhot[:, at])
             place = jnp.concatenate([chi_f[:, at]] * 2, axis=0)
             found = jnp.zeros((nq, step), F32)
             for i in range(LOW):
                 found = jnp.where(place == float(i), rows[i * nq:(i + 1) * nq], found)
-            picked[:, at] = found
-
-        @pl.loop(0, groups)
-        def _(h):
-            at = pl.ds(pl.multiple_of(h * 640, W), 640)
-            found = picked[:, at]
-            for i in range(8):
+            for i in range(each):
                 off = 80 * i % W
                 first = 80 * i // W
                 piece = found[:, first * W:(first + 1) * W]
@@ -250,10 +263,20 @@
                 if off + 80 > W:
                     other = pltpu.roll(found[:, (first + 1) * W:(first + 2) * W], W - off, 1)
                     piece = jnp.where(lane16 < W - off, piece, other)
-                send2[b, h * 8 + i] = jnp.where(lane16 < 80, piece, 0.0).astype(BF16)
+                send2[b, h * each + i] = jnp.where(lane16 < 80, piece, 0.0).astype(BF16)
+
+            @pl.loop(0, each)
+            def _(i):
+                e = h * each + lax.rem(i + f, each)
+
+                @pl.when(e != f)
+                def _():
+                    pltpu.make_async_remote_copy(
+                        src_ref=send2.at[b, e], dst_ref=recv2.at[b, f], send_sem=s2.at[b], recv_sem=r2.at[b],
+                        device_id={"fft": e}, device_id_type=MESH,
+                    ).start()
 
         recv2[b, f] = send2[b, f]
-        exchange(send2, recv2, s2, r2, b)
 
     nbr = 2 * nb * n_band
     swap = (
@@ -293,13 +316,13 @@
         whole = jnp.sum(part_recv[...], axis=0)[:, :nbr]
         coeffs = dot(coup_ref[g], whole, precision=lax.Precision.HIGHEST).astype(BF16).astype(F32)
         crossed = dot(coeffs, swap, precision=lax.Precision.HIGHEST)
-        factors = jnp.concatenate([coeffs, -crossed], axis=0).astype(BF16)
-
-        @pl.loop(0, SLOTS // 8)
+        factors = jnp.concatenate([coeffs, -crossed], axis=0).T.astype(BF16)
+
+        @pl.loop(0, SLOTS // 16)
         def _(m):
-            terms = dot(factors, beta_t[:, pl.ds(pl.multiple_of(m * 1024, 1024), 1024)], TN)
-            for i in range(8):
-                term_f[pl.ds(m * 8 + i, nbr, stride=PAD), :] = terms[:, i * W:(i + 1) * W]
+            terms = dot(factors, beta_t[:, pl.ds(pl.multiple_of(m * 2048, 2048), 2048)])
+            for i in range(16):
+                term_f[pl.ds(m * 16 + i, nbr, stride=PAD), :] = terms[:, i * W:(i + 1) * W]
 
         @pl.loop(0, n_band)
         def _(h):
@@ -316,6 +339,9 @@
                 device_id={"band": e}, device_id_type=MESH,
             ).start()
 
+    for load in loads[5:]:
+        load.wait()
+    diagonal()
     place_tables()
     potential_rows()
     projector_rows()
@@ -332,19 +358,22 @@
     expand()
     to_sticks(1)
 
-    gx, gy = colb[...] // W - RAD, colb[...] % W - RAD
-    kinetic = (gx * gx + gy * gy + wave_z * wave_z).astype(F32) / float(RAD * RAD)
     wait_bytes(term_recv.at[pl.ds(0, n_band - 1)], rn)
     for b in range(nb):
-        wait_bytes(recv2.at[b, pl.ds(0, n_fft - 1)], r2.at[b])
-        local = dot(recv2[b].reshape(n_fft * nq, W), z_tab[...], TN) * (1.0 / float(NG**3))
         for c in range(2):
             at = pl.ds((b * 2 + c) * SLOTS, SLOTS)
             nonlocal_sum = term_recv[0, at, :].astype(F32)
             for h in range(1, n_band):
                 nonlocal_sum = nonlocal_sum + term_recv[h, at, :].astype(F32)
-            wave = psi_ref[b, c].astype(F32) * in_sphere
-            out_ref[b, c] = in_sphere * (kinetic * wave + local[:SLOTS, c * W:(c + 1) * W] + nonlocal_sum)
+            base[b, c] = base[b, c] + in_sphere * nonlocal_sum
+
+    stores = [pltpu.make_async_copy(out_ref.at[b], out_h.at[b], out_sem.at[b]) for b in range(nb)]
+    for b in range(nb):
+        wait_bytes(recv2.at[b, pl.ds(0, n_fft - 1)], r2.at[b])
+        local = dot(recv2[b].reshape(n_fft * nq, W), z_tab[...], TN) * (1.0 / float(NG**3))
+        for c in range(2):
+            out_ref[b, c] = base[b, c] + in_sphere * local[:SLOTS, c * W:(c + 1) * W]
+        stores[b].start()
 
     for b in range(nb):
         wait_bytes(send1.at[b, pl.ds(0, n_fft - 1)], s1.at[b])
@@ -352,6 +381,8 @@
     wait_bytes(gath.at[pl.ds(0, n_band - 1)], sg)
     wait_bytes(part_recv.at[pl.ds(0, n_fft - 1)], sp)
     wait_bytes(term_send.at[pl.ds(0, n_band - 1)], sn)
+    for b in range(nb):
+        stores[b].wait()
 
 
 def body(n_band, n_fft, psi, stick_col, stick_len, plane_z, potential, beta, coupling):
@@ -360,15 +391,20 @@
     nq = 2 * PLANES
     nbr = 4 * n_band
     consts = [jnp.asarray(t) for t in tables()]
-    vmem = pl.BlockSpec(memory_space=pltpu.VMEM)
-    smem = pl.BlockSpec(memory_space=pltpu.SMEM)
+    hbm = pl.BlockSpec(memory_space=pl.ANY)
     dma = pltpu.SemaphoreType.DMA
+    operands = [
+        stick_len, stick_col, plane_z.reshape(1, n_slot), stick_col.reshape(tot // W, W),
+        psi, potential, beta, coupling, *consts,
+    ]
     return pl.pallas_call(
         functools.partial(kernel, n_band, n_fft),
         out_shape=jax.ShapeDtypeStruct(psi.shape, F32),
-        in_specs=[smem, smem] + [vmem] * 11,
-        out_specs=vmem,
+        in_specs=[hbm] * len(operands),
+        out_specs=hbm,
         scratch_shapes=[
+            *[(pltpu.SMEM if i < 2 else pltpu.VMEM)(x.shape, x.dtype) for i, x in enumerate(operands)],
+            pltpu.VMEM(psi.shape, F32),
             pltpu.VMEM((SLOTS, W), jnp.int32),
             pltpu.VMEM((SLOTS, W), jnp.int32),
             pltpu.VMEM((2, W, 2 * W), BF16),
@@ -395,16 +431,14 @@
             pltpu.VMEM((nbr * PAD, W), F32),
             pltpu.VMEM((n_band, 4 * SLOTS, W), BF16),
             pltpu.VMEM((n_band, 4 * SLOTS, W), BF16),
+            pltpu.VMEM(psi.shape, F32),
             dma((2,)), dma((2,)), dma((2,)), dma((2,)),
-            dma, dma, dma, dma, dma, dma,
+            dma, dma, dma, dma, dma, dma, dma((len(operands),)), dma((2,)),
         ],
         compiler_params=pltpu.CompilerParams(
             collective_id=0, has_side_effects=True, vmem_limit_bytes=56 * 1024 * 1024
         ),
-    )(
-        stick_len, stick_col, plane_z.reshape(1, n_slot), stick_col.reshape(tot // W, W),
-        psi, potential, beta, coupling, *consts,
-    )
+    )(*operands)
 
 
 def solution(mesh):

time: 47.6 us -> 43.7 us (0.918)
  Pallas kernels: 45.9 us -> 41.7 us
    pallas_call x1, Pallas kernels: 45.9 us -> 41.7 us  [body(): pl.pallas_call(functools.partial(kernel, n_band, n_fft), out_shape=jax.Sh...]
where the time goes in v2:
time: 43.7 us; the launch traced here: 43.3 us
  Pallas kernels  41.7 us (95%)
  local copies, waits for them, and re-layouts  1.59 us (4%)
    pallas_call x1, Pallas kernels, body(): pl.pallas_call(functools.partial(kernel, n_band, n_fft), out_shape=jax.Sh...  41.7 us
    unnamed x1, local copies, waits for them, and re-layouts  1.59 us

profile of v2, /device:TPU:16, one launch (start us, length us, event | category | flops | bytes accessed | tf_op | source)
XLA Modules:
  0.0 43.3 jit_solution(9232742206283105285)
XLA Ops:
  0.0 41.7 %shard_map.118 = f32[2,2,80,128]{3,2,1,0:T(8,128)} custom-call(s32[2560]{0:T(1024)} %len_h.1, s32[2560]{0:T(1024)} %col_h.1, s32[1,256]{1,0:T(1,128)} %bitcast.3, s32[20,128]{1,0:T(8,128)} %bitcast.2, bf16[2,2,80,128]{3,2,1,0:T(8,128)(2,1)} %psi_h.1, f32[8,57600]{1,0:T(8,128)} %pot_h.1, bf16[1,8,2,80,128]{4,3,2,1,0:T(8,128)(2,1)} %beta_h.1, ...), custom_call_target="tpu_custom_call" | custom-call | tf_op jit(solution)/shard_map/pallas_call | solution.py:400
  41.7 1.6 %copy.14 = f32[2,2,80,128]{3,2,1,0:T(8,128)} copy(f32[2,2,80,128]{3,2,1,0:T(8,128)} %shard_map.118) | data formatting | bytes 327680

commit v3 on v2

v3 whole, which is shorter than its diff:
```python
import functools
import math

import jax
import jax.numpy as jnp
import numpy as np
from jax import lax
from jax.experimental import pallas as pl
from jax.experimental.pallas import tpu as pltpu
from jax.sharding import PartitionSpec as P

NG = 240
RAD = 60
W = 128
SLOTS = 80
PLANES = 8
LOW = 64
PAD = 88
F32 = jnp.float32
BF16 = jnp.bfloat16
MESH = pl.DeviceIdType.MESH


def tables():
    wave = np.arange(W) - RAD
    pos = np.arange(256)
    angle = 2.0 * np.pi * ((wave[:, None] * pos[None, :]) % NG) / NG
    inside = (pos < NG)[None, :]
    co, si = np.cos(angle) * inside, np.sin(angle) * inside
    z_re = np.concatenate([co.T, -si.T], axis=1)
    z_im = np.concatenate([si.T, co.T], axis=1)
    y_out = np.block([[co, si], [-si, co]])
    y_back = y_out.T
    cx, sx = co[:, :NG].T, si[:, :NG].T
    x_out = np.block([[cx, -sx], [sx, cx]])
    x_out = x_out.reshape(2, NG // 16, 16, 2, W).transpose(1, 0, 2, 4, 3).reshape(2 * NG, 2 * W)
    x_back = x_out.T
    return [np.asarray(t, np.float32).astype(jnp.bfloat16) for t in (np.stack([z_re, z_im]), y_out, x_out, x_back, y_back)]


def iota(shape, dim):
    return lax.broadcasted_iota(jnp.int32, shape, dim)


def dot(a, b, dims=((1,), (0,)), precision=None):
    return lax.dot_general(a, b, (dims, ((), ())), preferred_element_type=F32, precision=precision)


NT = ((1,), (1,))
TN = ((0,), (0,))


def kernel(
    n_band, n_fft,
    len_h, col_h, plane_h, col2_h, len2_h, psi_h, pot_h, beta_h, coup_h, zt_h, yf_h, xf_h, xb_h, yb_h,
    out_h,
    len_s, col_s, plane_ref, col_ref, len_ref, psi_ref, pot_ref, beta_ref, coup_ref, zt_ref, yf_ref, xf_ref, xb_ref, yb_ref, out_ref,
    lenb, colb, psi2, z_tab, send1, recv1, send2, recv2,
    chi_f, chi_b, yhot, v3, dense, box, boxes, leave, come,
    gath, beta_other, beta_f, beta_t, psi_f, psi_t, product, part_send, part_recv, term_f, term_send, term_recv, base,
    s1, r1, s2, r2, sg, rg, sp, rp, sn, rn, sb, rb, load_sem, out_sem,
):
    f = lax.axis_index("fft")
    g = lax.axis_index("band")
    nb = 2
    tot = n_fft * SLOTS
    nq = 2 * PLANES
    cap = -(-tot // 2 // W) * W

    barrier = pltpu.get_barrier_semaphore()

    @pl.loop(1, n_fft)
    def _(k):
        pl.semaphore_signal(barrier, inc=1, device_id={"fft": lax.rem(f + k, n_fft)}, device_id_type=MESH)

    n_chip = n_band // 2
    chip = lax.div(g, 2)
    other = g + 1 - 2 * lax.rem(g, 2)

    def same_core(k):
        return lax.rem(g + 2 * k, n_band)

    pl.semaphore_signal(barrier, inc=1, device_id={"band": other}, device_id_type=MESH)
    for k in range(1, n_chip):
        pl.semaphore_signal(barrier, inc=1, device_id={"band": same_core(k)}, device_id_type=MESH)

    pairs = (
        (len_h, len_s), (col_h, col_s), (plane_h, plane_ref), (psi_h, psi_ref), (zt_h, zt_ref), (col2_h, col_ref), (len2_h, len_ref), (pot_h, pot_ref),
        (beta_h, beta_ref), (xf_h, xf_ref), (yf_h, yf_ref), (yb_h, yb_ref), (xb_h, xb_ref), (coup_h, coup_ref),
    )
    loads = [pltpu.make_async_copy(far, near, load_sem.at[i]) for i, (far, near) in enumerate(pairs)]
    for load in loads:
        load.start()
    for load in loads[:5]:
        load.wait()

    @pl.loop(0, SLOTS, unroll=8)
    def _(s):
        lenb[pl.ds(s, 1), :] = jnp.full((1, W), len_s[f * SLOTS + s], jnp.int32)
        colb[pl.ds(s, 1), :] = jnp.full((1, W), col_s[f * SLOTS + s], jnp.int32)

    wave_z = iota((SLOTS, W), 1) - RAD
    in_sphere = (2 * jnp.abs(wave_z) < lenb[...]).astype(F32)
    psi2[...] = jnp.zeros(psi2.shape, BF16)
    for b in range(nb):
        for c in range(2):
            psi2[b, 0:SLOTS, c * W:(c + 1) * W] = (psi_ref[b, c].astype(F32) * in_sphere).astype(BF16)

    n_slot = n_fft * PLANES
    hot_z = (iota((256, n_slot), 0) == plane_ref[...]).astype(F32).T.astype(BF16)
    z_re = dot(hot_z, zt_ref[0]).reshape(n_fft, 1, PLANES, 256)
    z_im = dot(hot_z, zt_ref[1]).reshape(n_fft, 1, PLANES, 256)
    z_tab[...] = jnp.concatenate([z_re, z_im], axis=1).reshape(n_fft * nq, 256).astype(BF16)
    for b in range(nb):
        along = dot(z_tab[...], psi2[b], NT)
        send1[b] = along.reshape(n_fft, nq, W).astype(BF16)
        recv1[b, f] = send1[b, f]

    pl.semaphore_wait(barrier, n_fft - 1 + n_chip)

    def exchange(send, recv, send_sem, recv_sem, b):
        @pl.loop(1, n_fft)
        def _(k):
            e = lax.rem(f + k, n_fft)
            pltpu.make_async_remote_copy(
                src_ref=send.at[b, e], dst_ref=recv.at[b, f], send_sem=send_sem.at[b], recv_sem=recv_sem.at[b],
                device_id={"fft": e}, device_id_type=MESH,
            ).start()

    def wait_bytes(ref, sem):
        pltpu.make_async_copy(ref, ref, sem).wait()

    exchange(send1, recv1, s1, r1, 0)

    def to_chips(k, src, dst, send_sem, recv_sem):
        return pltpu.make_async_remote_copy(
            src_ref=src, dst_ref=dst, send_sem=send_sem, recv_sem=recv_sem,
            device_id={"band": same_core(k)}, device_id_type=MESH,
        )

    for k in range(1, n_chip):
        to_chips(k, psi_ref, gath.at[chip], sg, rg).start()
    loads[8].wait()
    swap_beta = pltpu.make_async_remote_copy(
        src_ref=beta_ref, dst_ref=beta_other, send_sem=sb, recv_sem=rb, device_id={"band": other}, device_id_type=MESH
    )
    swap_beta.start()
    gath[chip] = psi_ref[...]

    bits = (n_fft * W - 1).bit_length()
    lane8 = iota((8, W), 1)

    def moved_left(cols, k):
        if k >= 7:
            far = 1 << (k - 7)
            return cols[far:] + [jnp.zeros_like(cols[0])] * min(far, len(cols))
        step = 1 << k
        rolled = [pltpu.roll(col, W - step, 1) for col in cols]
        lane = iota(cols[0].shape, 1)
        return [jnp.where(lane < W - step, one, two) for one, two in zip(rolled, rolled[1:] + [jnp.zeros_like(cols[0])])]

    def moved_right(cols, k):
        if k >= 7:
            far = 1 << (k - 7)
            return [jnp.zeros_like(cols[0])] * min(far, len(cols)) + cols[:max(len(cols) - far, 0)]
        step = 1 << k
        rolled = [pltpu.roll(col, step, 1) for col in cols]
        lane = iota(cols[0].shape, 1)
        return [jnp.where(lane >= step, one, two) for one, two in zip(rolled, [jnp.zeros_like(cols[0])] + rolled[:-1])]

    def place_tables():
        dense = []
        for r in range(tot // W):
            used = jnp.broadcast_to(len_ref[r:r + 1, :], (8, W)) > 0
            dense.append(jnp.where(used, jnp.broadcast_to(col_ref[r:r + 1, :], (8, W)), -1))
        cols, moves = [], []
        ahead = jnp.zeros((8, 1), F32)
        for e in range(n_fft):
            first, off = 80 * e // W, 80 * e % W
            piece = pltpu.roll(dense[first], W - off, 1) if off else dense[first]
            if off + 80 > W:
                piece = jnp.where(lane8 < W - off, piece, pltpu.roll(dense[first + 1], W - off, 1))
            piece = jnp.where(lane8 < 80, piece, -1)
            used = piece >= 0
            cols.append(piece)
            moves.append(jnp.where(used, jnp.broadcast_to(ahead, (8, W)), 0.0).astype(jnp.int32))
            ahead = ahead + (float(W) - jnp.sum(used.astype(F32), axis=1, keepdims=True))
        for k in range(bits):
            next_moves, next_cols = moved_left(moves, k), moved_left(cols, k)
            for e in range(n_fft):
                leaves, comes = (moves[e] >> k) & 1, (next_moves[e] >> k) & 1
                at = slice(e * W, (e + 1) * W)
                leave[k, :, at] = leaves
                come[k, :, at] = comes
                moves[e] = jnp.where(comes > 0, next_moves[e], jnp.where(leaves > 0, 0, moves[e]))
                cols[e] = jnp.where(comes > 0, next_cols[e], jnp.where(leaves > 0, -1, cols[e]))
        for r in range(cap // W):
            at = slice(r * W, (r + 1) * W)
            c, d = cols[r] >> 7, cols[r] & (W - 1)
            chi = (c & (LOW - 1)).astype(F32)
            chi_f[:, at] = chi
            chi_b[:, at] = jnp.concatenate([chi, chi], axis=0).astype(BF16)
            row = jnp.where(cols[r] < 0, -1, (c >> 6) * W + d)
            yhot[:, at] = (iota((2 * W, W), 0) == row[:1]).astype(F32).astype(BF16)

    def diagonal():
        gx, gy = colb[...] // W - RAD, colb[...] % W - RAD
        kinetic = (gx * gx + gy * gy + wave_z * wave_z).astype(F32) / float(RAD * RAD)
        for b in range(nb):
            for c in range(2):
                base[b, c] = kinetic * in_sphere * psi_ref[b, c].astype(F32)

    def potential_rows():
        @pl.loop(0, NG // 24)
        def _(m3):
            for u in range(3):
                m = m3 * 3 + u
                for r in range(8):
                    start = 240 * r
                    low = start // W * W
                    width = 256 if start - low <= 16 else 384
                    piece = pot_ref[:, pl.ds(pl.multiple_of(m * 1920 + low, W), width)]
                    if start - low:
                        piece = pltpu.roll(piece, width - (start - low), 1)
                    for c in range(2):
                        v3[c, pl.ds(pl.multiple_of((m * 8 + r) * 8, 8), 8), :] = piece[:, c * W:(c + 1) * W]

    def projector_rows():
        swap_beta.wait_recv()
        for a, source in enumerate((beta_ref, beta_other)):
            for k in range(8):
                for c in range(2):
                    beta_f[pl.ds((c * 16 + a * 8 + k) * PAD, SLOTS), :] = source[0, k, c].astype(F32) * in_sphere

        @pl.loop(0, SLOTS // 4)
        def _(s4):
            for u in range(4):
                s = s4 * 4 + u
                rows = beta_f[pl.ds(s, 32, stride=PAD), :]
                beta_t[:, pl.ds(pl.multiple_of(s * W, W), W)] = rows.astype(BF16)

    def to_planes(b):
        wait_bytes(recv1.at[b, pl.ds(0, n_fft - 1)], r1.at[b])

    def both(mask):
        return jnp.concatenate([mask, mask], axis=0)

    def pack_sticks(b):
        cols = [recv1[b, e].astype(F32) for e in range(n_fft)]
        for k in range(bits):
            arriving = moved_left(cols, k)
            cols = [jnp.where(both(come[k, :, e * W:(e + 1) * W]) > 0, arriving[e], cols[e]) for e in range(n_fft)]
        dense[...] = jnp.concatenate(cols[:cap // W], axis=1).astype(BF16)

    def place_columns(b):
        sticks, place = dense[...], chi_b[...]
        rows = [jnp.where(place == jnp.asarray(i, BF16), sticks, jnp.asarray(0, BF16)) for i in range(LOW)]
        placed = dot(jnp.concatenate(rows, axis=0), yhot[...], NT)
        for h in range(2):
            box[h] = placed[:, h * W:(h + 1) * W]

    def transform():
        @pl.loop(0, PLANES // 4)
        def _(quad):
            along_x = []
            for p in range(2):
                pair = []
                for u in range(2):
                    t = quad * 4 + p * 2 + u
                    pair.append(jnp.concatenate([box[h, pl.ds(t, W, stride=PLANES), :] for h in range(2)], axis=0))
                wide = dot(xf_ref[...], jnp.concatenate(pair, axis=1).astype(BF16)).astype(BF16)
                wide = wide.reshape(NG // 16, 2, 16, 2 * W)
                for u in range(2):
                    part = [wide[:, c, :, u * W:(u + 1) * W].reshape(NG, W) for c in range(2)]
                    along_x.append(jnp.concatenate(part, axis=1))
            full = dot(jnp.concatenate(along_x, axis=0), yf_ref[...])
            weighted = []
            for u in range(4):
                weight = [v3[c, pl.ds(quad * 4 + u, NG, stride=PLANES), :] for c in range(2)]
                weighted.append((full[u * NG:(u + 1) * NG] * jnp.concatenate(weight * 2, axis=1)).astype(BF16))
            back = dot(jnp.concatenate(weighted, axis=0), yb_ref[...]).astype(BF16)
            for p in range(2):
                pair = [back[(p * 2 + u) * NG:(p * 2 + u + 1) * NG] for u in range(2)]
                pair = [part.reshape(NG // 16, 1, 16, 2 * W) for part in pair]
                pair = [jnp.concatenate([part[..., :W], part[..., W:]], axis=1).reshape(2 * NG, W) for part in pair]
                wide = dot(xb_ref[...], jnp.concatenate(pair, axis=1))
                for u in range(2):
                    t = quad * 4 + p * 2 + u
                    for h in range(2):
                        box[h, pl.ds(t, W, stride=PLANES), :] = wide[h * W:(h + 1) * W, u * W:(u + 1) * W]

    def to_sticks(b):
        boxes[...] = jnp.concatenate([box[0], box[1]], axis=1).astype(BF16)

        rows = dot(boxes[...], yhot[...])
        place = both(chi_f[...])
        found = jnp.zeros((nq, cap), F32)
        for i in range(LOW):
            found = jnp.where(place == float(i), rows[i * nq:(i + 1) * nq], found)
        cols = [found[:, r * W:(r + 1) * W] for r in range(cap // W)]
        cols = cols + [jnp.zeros((nq, W), F32)] * (n_fft - len(cols))
        for k in reversed(range(bits)):
            leaving = moved_right(cols, k)
            cols = [jnp.where(both(leave[k, :, e * W:(e + 1) * W]) > 0, leaving[e], cols[e]) for e in range(n_fft)]
        for e in range(n_fft):
            send2[b, e] = cols[e].astype(BF16)
        recv2[b, f] = send2[b, f]
        exchange(send2, recv2, s2, r2, b)

    nbr = 2 * nb * n_chip

    def cross(x):
        return jnp.where(iota(x.shape, 1) % 2 == 0, pltpu.roll(x, W - 1, 1), -pltpu.roll(x, 1, 1))

    def project():
        if n_chip > 1:
            wait_bytes(gath.at[pl.ds(0, n_chip - 1)], rg)

        @pl.loop(0, n_chip)
        def _(h):
            for b in range(nb):
                for c in range(2):
                    psi_f[pl.ds(pl.multiple_of((h * 4 + b * 2 + c) * PAD, 8), SLOTS), :] = gath[h, b, c].astype(F32)

        @pl.loop(0, SLOTS // 8)
        def _(s8):
            for u in range(8):
                s = s8 * 8 + u
                psi_t[:, pl.ds(pl.multiple_of(s * W, W), W)] = psi_f[pl.ds(s, nbr, stride=PAD), :].astype(BF16)

        product[...] = jnp.zeros(product.shape, F32)
        product[:, :nbr] = dot(beta_t[...], psi_t[...], NT)
        one, two = [product[a * 8:a * 8 + 8] + cross(product[16 + a * 8:24 + a * 8]) for a in range(2)]
        part_send[...] = jnp.where(lane8 < nbr, one, pltpu.roll(two, nbr, 1))
        part_recv[f] = part_send[...]

        @pl.loop(1, n_fft)
        def _(k):
            pltpu.make_async_remote_copy(
                src_ref=part_send, dst_ref=part_recv.at[f], send_sem=sp, recv_sem=rp,
                device_id={"fft": lax.rem(f + k, n_fft)}, device_id_type=MESH,
            ).start()

    def expand():
        wait_bytes(part_recv.at[pl.ds(0, n_fft - 1)], rp)
        whole = jnp.sum(part_recv[...], axis=0)
        coupling = jnp.concatenate([coup_ref[g], coup_ref[other]], axis=0)
        coupled = dot(coupling, whole, precision=lax.Precision.HIGHEST)
        coeffs = jnp.where(lane8 < nbr, coupled[:8], coupled[8:]).astype(BF16).astype(F32)
        crossed = -cross(coeffs)
        factors = [x if a == 0 else pltpu.roll(x, W - nbr, 1) for x in (coeffs, crossed) for a in range(2)]
        factors = jnp.concatenate(factors + [jnp.zeros((W - 32, W), F32)], axis=0).T[:nbr, :32].astype(BF16)

        @pl.loop(0, SLOTS // 16)
        def _(m):
            terms = dot(factors, beta_t[:, pl.ds(pl.multiple_of(m * 2048, 2048), 2048)])
            for i in range(16):
                term_f[pl.ds(m * 16 + i, nbr, stride=PAD), :] = terms[:, i * W:(i + 1) * W]

        for k in reversed(range(n_chip)):
            h = lax.div(same_core(k), 2)
            for i in range(4):
                at = pl.ds(pl.multiple_of((h * 4 + i) * PAD, 8), SLOTS)
                term_send[h, i * SLOTS:(i + 1) * SLOTS, :] = term_f[at, :].astype(BF16)
            if k:
                to_chips(k, term_send.at[h], term_recv.at[chip], sn, rn).start()
            else:
                term_recv[chip] = term_send[chip]

    for load in loads[5:8] + loads[9:]:
        load.wait()
    diagonal()
    place_tables()
    potential_rows()
    projector_rows()
    to_planes(0)
    exchange(send1, recv1, s1, r1, 1)
    pack_sticks(0)
    place_columns(0)
    project()
    transform()
    to_sticks(0)
    to_planes(1)
    pack_sticks(1)
    place_columns(1)
    transform()
    expand()
    to_sticks(1)

    if n_chip > 1:
        wait_bytes(term_recv.at[pl.ds(0, n_chip - 1)], rn)
    for b in range(nb):
        for c in range(2):
            at = pl.ds((b * 2 + c) * SLOTS, SLOTS)
            nonlocal_sum = term_recv[0, at, :].astype(F32)
            for h in range(1, n_chip):
                nonlocal_sum = nonlocal_sum + term_recv[h, at, :].astype(F32)
            base[b, c] = base[b, c] + in_sphere * nonlocal_sum

    stores = [pltpu.make_async_copy(out_ref.at[b], out_h.at[b], out_sem.at[b]) for b in range(nb)]
    for b in range(nb):
        wait_bytes(recv2.at[b, pl.ds(0, n_fft - 1)], r2.at[b])
        local = dot(recv2[b].reshape(n_fft * nq, W), z_tab[...], TN) * (1.0 / float(NG**3))
        for c in range(2):
            out_ref[b, c] = base[b, c] + in_sphere * local[:SLOTS, c * W:(c + 1) * W]
        stores[b].start()

    for b in range(nb):
        wait_bytes(send1.at[b, pl.ds(0, n_fft - 1)], s1.at[b])
        wait_bytes(send2.at[b, pl.ds(0, n_fft - 1)], s2.at[b])
    if n_chip > 1:
        wait_bytes(gath.at[pl.ds(0, n_chip - 1)], sg)
        wait_bytes(term_send.at[pl.ds(0, n_chip - 1)], sn)
    wait_bytes(part_recv.at[pl.ds(0, n_fft - 1)], sp)
    swap_beta.wait_send()
    for b in range(nb):
        stores[b].wait()


def body(n_band, n_fft, psi, stick_col, stick_len, plane_z, potential, beta, coupling):
    tot = n_fft * SLOTS
    n_slot = n_fft * PLANES
    nq = 2 * PLANES
    n_chip = n_band // 2
    nbr = 4 * n_chip
    cap = -(-tot // 2 // W) * W
    consts = [jnp.asarray(t) for t in tables()]
    hbm = pl.BlockSpec(memory_space=pl.ANY)
    dma = pltpu.SemaphoreType.DMA
    operands = [
        stick_len, stick_col, plane_z.reshape(1, n_slot), stick_col.reshape(tot // W, W), stick_len.reshape(tot // W, W),
        psi, potential, beta, coupling, *consts,
    ]
    return pl.pallas_call(
        functools.partial(kernel, n_band, n_fft),
        out_shape=jax.ShapeDtypeStruct(psi.shape, F32),
        in_specs=[hbm] * len(operands),
        out_specs=hbm,
        scratch_shapes=[
            *[(pltpu.SMEM if i < 2 else pltpu.VMEM)(x.shape, x.dtype) for i, x in enumerate(operands)],
            pltpu.VMEM(psi.shape, F32),
            pltpu.VMEM((SLOTS, W), jnp.int32),
            pltpu.VMEM((SLOTS, W), jnp.int32),
            pltpu.VMEM((2, W, 2 * W), BF16),
            pltpu.VMEM((n_fft * nq, 2 * W), BF16),
            pltpu.VMEM((2, n_fft, nq, W), BF16),
            pltpu.VMEM((2, n_fft, nq, W), BF16),
            pltpu.VMEM((2, n_fft, nq, W), BF16),
            pltpu.VMEM((2, n_fft, nq, W), BF16),
            pltpu.VMEM((8, cap), F32),
            pltpu.VMEM((nq, cap), BF16),
            pltpu.VMEM((2 * W, cap), BF16),
            pltpu.VMEM((2, NG * PLANES, W), F32),
            pltpu.VMEM((nq, cap), BF16),
            pltpu.VMEM((2, LOW * nq, W), F32),
            pltpu.VMEM((LOW * nq, 2 * W), BF16),
            pltpu.VMEM(((n_fft * W - 1).bit_length(), 8, n_fft * W), jnp.int32),
            pltpu.VMEM(((n_fft * W - 1).bit_length(), 8, n_fft * W), jnp.int32),
            pltpu.VMEM((n_chip, 2, 2, SLOTS, W), BF16),
            pltpu.VMEM(beta.shape, BF16),
            pltpu.VMEM((32 * PAD, W), F32),
            pltpu.VMEM((32, SLOTS * W), BF16),
            pltpu.VMEM((nbr * PAD, W), F32),
            pltpu.VMEM((nbr, SLOTS * W), BF16),
            pltpu.VMEM((32, W), F32),
            pltpu.VMEM((8, W), F32),
            pltpu.VMEM((n_fft, 8, W), F32),
            pltpu.VMEM((nbr * PAD, W), F32),
            pltpu.VMEM((n_chip, 4 * SLOTS, W), BF16),
            pltpu.VMEM((n_chip, 4 * SLOTS, W), BF16),
            pltpu.VMEM(psi.shape, F32),
            dma((2,)), dma((2,)), dma((2,)), dma((2,)),
            dma, dma, dma, dma, dma, dma, dma, dma, dma((len(operands),)), dma((2,)),
        ],
        compiler_params=pltpu.CompilerParams(
            collective_id=0, has_side_effects=True, vmem_limit_bytes=56 * 1024 * 1024
        ),
    )(*operands)


def solution(mesh):
    in_specs = (
        P("band", None, "fft", None),
        P(),
        P(),
        P(),
        P("fft", None),
        P("band", None, None, "fft", None),
        P(),
    )
    out_specs = P("band", None, "fft", None)
    part = functools.partial(body, mesh.shape["band"], mesh.shape["fft"])
    return jax.shard_map(part, mesh=mesh, in_specs=in_specs, out_specs=out_specs, check_vma=False)
```

time: 43.7 us -> 41 us (0.938)
  Pallas kernels: 41.7 us -> 39.2 us
    pallas_call x1, Pallas kernels: 41.7 us -> 39.2 us  [body(): pl.pallas_call(functools.partial(kernel, n_band, n_fft), out_shape=jax.Sh...]
where the time goes in v3:
time: 41 us; the launch traced here: 40.8 us
  Pallas kernels  39.2 us (96%)
  local copies, waits for them, and re-layouts  1.59 us (4%)
    pallas_call x1, Pallas kernels, body(): pl.pallas_call(functools.partial(kernel, n_band, n_fft), out_shape=jax.Sh...  39.2 us
    unnamed x1, local copies, waits for them, and re-layouts  1.59 us

profile of v3, /device:TPU:16, one launch (start us, length us, event | category | flops | bytes accessed | tf_op | source)
XLA Modules:
  0.0 40.8 jit_solution(5585739532077211135)
XLA Ops:
  0.0 39.2 %shard_map.118 = f32[2,2,80,128]{3,2,1,0:T(8,128)} custom-call(s32[2560]{0:T(1024)} %len_h.1, s32[2560]{0:T(1024)} %col_h.1, s32[1,256]{1,0:T(1,128)} %bitcast.5, s32[20,128]{1,0:T(8,128)} %bitcast.4, s32[20,128]{1,0:T(8,128)} %bitcast.3, bf16[2,2,80,128]{3,2,1,0:T(8,128)(2,1)} %psi_h.1, f32[8,57600]{1,0:T(8,128)} %pot_h.1, ...), custom_call_target="tpu_custom_call" | custom-call | tf_op jit(solution)/shard_map/pallas_call | solution.py:434
  39.3 1.6 %copy.14 = f32[2,2,80,128]{3,2,1,0:T(8,128)} copy(f32[2,2,80,128]{3,2,1,0:T(8,128)} %shard_map.118) | data formatting | bytes 327680

commit v4 on v3

--- a/solution.py
+++ b/solution.py
@@ -67,11 +67,25 @@
     nq = 2 * PLANES
     cap = -(-tot // 2 // W) * W
 
+    def others_along_fft(start):
+        n_x = n_fft // 8
+        steps = [n_x // 2] + [n_x // 2 + sign * d for d in range(1, n_x // 2 + 1) for sign in (-1, 1) if n_x // 2 + sign * d < n_x]
+        x, z = f >> 3, f & 7
+
+        @pl.loop(0, 7)
+        def _(j):
+            half = (j + 1) >> 1
+            to_z = (z + 4 + jnp.where((j & 1) == 1, -half, half)) & 7
+            for step in steps:
+                start((((x + step) & (n_x - 1)) << 3) + to_z)
+
+        for step in steps:
+            if step:
+                start((((x + step) & (n_x - 1)) << 3) + z)
+
     barrier = pltpu.get_barrier_semaphore()
 
-    @pl.loop(1, n_fft)
-    def _(k):
-        pl.semaphore_signal(barrier, inc=1, device_id={"fft": lax.rem(f + k, n_fft)}, device_id_type=MESH)
+    others_along_fft(lambda e: pl.semaphore_signal(barrier, inc=1, device_id={"fft": e}, device_id_type=MESH))
 
     n_chip = n_band // 2
     chip = lax.div(g, 2)
@@ -119,13 +133,13 @@
     pl.semaphore_wait(barrier, n_fft - 1 + n_chip)
 
     def exchange(send, recv, send_sem, recv_sem, b):
-        @pl.loop(1, n_fft)
-        def _(k):
-            e = lax.rem(f + k, n_fft)
+        def start(e):
             pltpu.make_async_remote_copy(
                 src_ref=send.at[b, e], dst_ref=recv.at[b, f], send_sem=send_sem.at[b], recv_sem=recv_sem.at[b],
                 device_id={"fft": e}, device_id_type=MESH,
             ).start()
+
+        others_along_fft(start)
 
     def wait_bytes(ref, sem):
         pltpu.make_async_copy(ref, ref, sem).wait()
@@ -371,10 +385,10 @@
         load.wait()
     diagonal()
     place_tables()
+    exchange(send1, recv1, s1, r1, 1)
     potential_rows()
     projector_rows()
     to_planes(0)
-    exchange(send1, recv1, s1, r1, 1)
     pack_sticks(0)
     place_columns(0)
     project()

time: 41 us -> 39.1 us (0.954)
  Pallas kernels: 39.2 us -> 37.3 us
    pallas_call x1, Pallas kernels: 39.2 us -> 37.3 us  [body(): pl.pallas_call(functools.partial(kernel, n_band, n_fft), out_shape=jax.Sh...]
where the time goes in v4:
time: 39.1 us; the launch traced here: 38.9 us
  Pallas kernels  37.3 us (95%)
  local copies, waits for them, and re-layouts  1.59 us (4%)
    pallas_call x1, Pallas kernels, body(): pl.pallas_call(functools.partial(kernel, n_band, n_fft), out_shape=jax.Sh...  37.3 us
    unnamed x1, local copies, waits for them, and re-layouts  1.59 us

profile of v4, /device:TPU:16, one launch (start us, length us, event | category | flops | bytes accessed | tf_op | source)
XLA Modules:
  0.0 38.9 jit_solution(4790668482411835613)
XLA Ops:
  0.0 37.3 %shard_map.118 = f32[2,2,80,128]{3,2,1,0:T(8,128)} custom-call(s32[2560]{0:T(1024)} %len_h.1, s32[2560]{0:T(1024)} %col_h.1, s32[1,256]{1,0:T(1,128)} %bitcast.5, s32[20,128]{1,0:T(8,128)} %bitcast.4, s32[20,128]{1,0:T(8,128)} %bitcast.3, bf16[2,2,80,128]{3,2,1,0:T(8,128)(2,1)} %psi_h.1, f32[8,57600]{1,0:T(8,128)} %pot_h.1, ...), custom_call_target="tpu_custom_call" | custom-call | tf_op jit(solution)/shard_map/pallas_call | solution.py:448
  37.4 1.6 %copy.14 = f32[2,2,80,128]{3,2,1,0:T(8,128)} copy(f32[2,2,80,128]{3,2,1,0:T(8,128)} %shard_map.118) | data formatting | bytes 327680

commit v5 on v4

--- a/solution.py
+++ b/solution.py
@@ -303,9 +303,11 @@
                     for h in range(2):
                         box[h, pl.ds(t, W, stride=PLANES), :] = wide[h * W:(h + 1) * W, u * W:(u + 1) * W]
 
-    def to_sticks(b):
+    def to_sticks(b, beside=None, after=None):
         boxes[...] = jnp.concatenate([box[0], box[1]], axis=1).astype(BF16)
 
+        if beside is not None:
+            beside()
         rows = dot(boxes[...], yhot[...])
         place = both(chi_f[...])
         found = jnp.zeros((nq, cap), F32)
@@ -318,6 +320,8 @@
             cols = [jnp.where(both(leave[k, :, e * W:(e + 1) * W]) > 0, leaving[e], cols[e]) for e in range(n_fft)]
         for e in range(n_fft):
             send2[b, e] = cols[e].astype(BF16)
+        if after is not None:
+            after()
         recv2[b, f] = send2[b, f]
         exchange(send2, recv2, s2, r2, b)
 
@@ -326,22 +330,17 @@
     def cross(x):
         return jnp.where(iota(x.shape, 1) % 2 == 0, pltpu.roll(x, W - 1, 1), -pltpu.roll(x, 1, 1))
 
-    def project():
+    def psi_rows():
         if n_chip > 1:
             wait_bytes(gath.at[pl.ds(0, n_chip - 1)], rg)
-
-        @pl.loop(0, n_chip)
-        def _(h):
+        for h in range(n_chip):
             for b in range(nb):
                 for c in range(2):
-                    psi_f[pl.ds(pl.multiple_of((h * 4 + b * 2 + c) * PAD, 8), SLOTS), :] = gath[h, b, c].astype(F32)
-
-        @pl.loop(0, SLOTS // 8)
-        def _(s8):
-            for u in range(8):
-                s = s8 * 8 + u
-                psi_t[:, pl.ds(pl.multiple_of(s * W, W), W)] = psi_f[pl.ds(s, nbr, stride=PAD), :].astype(BF16)
-
+                    psi_f[pl.ds((h * 4 + b * 2 + c) * PAD, SLOTS), :] = gath[h, b, c].astype(F32)
+        for s in range(SLOTS):
+            psi_t[:, s * W:(s + 1) * W] = psi_f[pl.ds(s, nbr, stride=PAD), :].astype(BF16)
+
+    def project():
         product[...] = jnp.zeros(product.shape, F32)
         product[:, :nbr] = dot(beta_t[...], psi_t[...], NT)
         one, two = [product[a * 8:a * 8 + 8] + cross(product[16 + a * 8:24 + a * 8]) for a in range(2)]
@@ -355,7 +354,7 @@
                 device_id={"fft": lax.rem(f + k, n_fft)}, device_id_type=MESH,
             ).start()
 
-    def expand():
+    def term_factors():
         wait_bytes(part_recv.at[pl.ds(0, n_fft - 1)], rp)
         whole = jnp.sum(part_recv[...], axis=0)
         coupling = jnp.concatenate([coup_ref[g], coup_ref[other]], axis=0)
@@ -365,12 +364,15 @@
         factors = [x if a == 0 else pltpu.roll(x, W - nbr, 1) for x in (coeffs, crossed) for a in range(2)]
         factors = jnp.concatenate(factors + [jnp.zeros((W - 32, W), F32)], axis=0).T[:nbr, :32].astype(BF16)
 
-        @pl.loop(0, SLOTS // 16)
-        def _(m):
-            terms = dot(factors, beta_t[:, pl.ds(pl.multiple_of(m * 2048, 2048), 2048)])
+        return factors
+
+    def expand_rows(factors):
+        for m in range(SLOTS // 16):
+            terms = dot(factors, beta_t[:, m * 2048:(m + 1) * 2048])
             for i in range(16):
                 term_f[pl.ds(m * 16 + i, nbr, stride=PAD), :] = terms[:, i * W:(i + 1) * W]
 
+    def send_terms():
         for k in reversed(range(n_chip)):
             h = lax.div(same_core(k), 2)
             for i in range(4):
@@ -389,35 +391,50 @@
     potential_rows()
     projector_rows()
     to_planes(0)
+    psi_rows()
     pack_sticks(0)
     place_columns(0)
     project()
     transform()
-    to_sticks(0)
     to_planes(1)
-    pack_sticks(1)
-    place_columns(1)
+
+    def next_band():
+        pack_sticks(1)
+        place_columns(1)
+
+    to_sticks(0, after=next_band)
     transform()
-    expand()
-    to_sticks(1)
-
+    factors = term_factors()
+    to_sticks(1, lambda: expand_rows(factors))
+    send_terms()
+
+    def local_term(b):
+        wait_bytes(recv2.at[b, pl.ds(0, n_fft - 1)], r2.at[b])
+        local = dot(recv2[b].reshape(n_fft * nq, W), z_tab[...], TN) * (1.0 / float(NG**3))
+        return [in_sphere * local[:SLOTS, c * W:(c + 1) * W] for c in range(2)]
+
+    first = local_term(0)
+    for c in range(2):
+        out_ref[0, c] = base[0, c] + first[c]
     if n_chip > 1:
         wait_bytes(term_recv.at[pl.ds(0, n_chip - 1)], rn)
+    stores = [pltpu.make_async_copy(out_ref.at[b], out_h.at[b], out_sem.at[b]) for b in range(nb)]
     for b in range(nb):
         for c in range(2):
             at = pl.ds((b * 2 + c) * SLOTS, SLOTS)
             nonlocal_sum = term_recv[0, at, :].astype(F32)
             for h in range(1, n_chip):
                 nonlocal_sum = nonlocal_sum + term_recv[h, at, :].astype(F32)
-            base[b, c] = base[b, c] + in_sphere * nonlocal_sum
-
-    stores = [pltpu.make_async_copy(out_ref.at[b], out_h.at[b], out_sem.at[b]) for b in range(nb)]
-    for b in range(nb):
-        wait_bytes(recv2.at[b, pl.ds(0, n_fft - 1)], r2.at[b])
-        local = dot(recv2[b].reshape(n_fft * nq, W), z_tab[...], TN) * (1.0 / float(NG**3))
-        for c in range(2):
-            out_ref[b, c] = base[b, c] + in_sphere * local[:SLOTS, c * W:(c + 1) * W]
-        stores[b].start()
+            if b == 0:
+                out_ref[b, c] = out_ref[b, c] + in_sphere * nonlocal_sum
+            else:
+                base[b, c] = base[b, c] + in_sphere * nonlocal_sum
+        if b == 0:
+            stores[b].start()
+    second = local_term(1)
+    for c in range(2):
+        out_ref[1, c] = base[1, c] + second[c]
+    stores[1].start()
 
     for b in range(nb):
         wait_bytes(send1.at[b, pl.ds(0, n_fft - 1)], s1.at[b])

time: 39.1 us -> 36 us (0.921)
  Pallas kernels: 37.3 us -> 34.3 us
    pallas_call x1, Pallas kernels: 37.3 us -> 34.3 us  [body(): pl.pallas_call(functools.partial(kernel, n_band, n_fft), out_shape=jax.Sh...]
where the time goes in v5:
time: 36 us; the launch traced here: 35.9 us
  Pallas kernels  34.3 us (95%)
  local copies, waits for them, and re-layouts  1.59 us (4%)
    pallas_call x1, Pallas kernels, body(): pl.pallas_call(functools.partial(kernel, n_band, n_fft), out_shape=jax.Sh...  34.3 us
    unnamed x1, local copies, waits for them, and re-layouts  1.59 us

profile of v5, /device:TPU:16, one launch (start us, length us, event | category | flops | bytes accessed | tf_op | source)
XLA Modules:
  0.0 35.9 jit_solution(573858624630515866)
XLA Ops:
  0.0 34.3 %shard_map.118 = f32[2,2,80,128]{3,2,1,0:T(8,128)} custom-call(s32[2560]{0:T(1024)} %len_h.1, s32[2560]{0:T(1024)} %col_h.1, s32[1,256]{1,0:T(1,128)} %bitcast.5, s32[20,128]{1,0:T(8,128)} %bitcast.4, s32[20,128]{1,0:T(8,128)} %bitcast.3, bf16[2,2,80,128]{3,2,1,0:T(8,128)(2,1)} %psi_h.1, f32[8,57600]{1,0:T(8,128)} %pot_h.1, ...), custom_call_target="tpu_custom_call" | custom-call | tf_op jit(solution)/shard_map/pallas_call | solution.py:465
  34.3 1.6 %copy.14 = f32[2,2,80,128]{3,2,1,0:T(8,128)} copy(f32[2,2,80,128]{3,2,1,0:T(8,128)} %shard_map.118) | data formatting | bytes 327680

commit v6 on v5

--- a/solution.py
+++ b/solution.py
@@ -161,8 +161,12 @@
     swap_beta.start()
     gath[chip] = psi_ref[...]
 
+    def both(mask):
+        return jnp.concatenate([mask, mask], axis=0)
+
     bits = (n_fft * W - 1).bit_length()
     lane8 = iota((8, W), 1)
+    lane16 = iota((nq, W), 1).astype(F32).astype(BF16)
 
     def moved_left(cols, k):
         if k >= 7:
@@ -170,8 +174,8 @@
             return cols[far:] + [jnp.zeros_like(cols[0])] * min(far, len(cols))
         step = 1 << k
         rolled = [pltpu.roll(col, W - step, 1) for col in cols]
-        lane = iota(cols[0].shape, 1)
-        return [jnp.where(lane < W - step, one, two) for one, two in zip(rolled, rolled[1:] + [jnp.zeros_like(cols[0])])]
+        lane = lane16 if cols[0].dtype == BF16 else lane8
+        return [jnp.where(lane < jnp.asarray(W - step, lane.dtype), one, two) for one, two in zip(rolled, rolled[1:] + [jnp.zeros_like(cols[0])])]
 
     def moved_right(cols, k):
         if k >= 7:
@@ -179,8 +183,8 @@
             return [jnp.zeros_like(cols[0])] * min(far, len(cols)) + cols[:max(len(cols) - far, 0)]
         step = 1 << k
         rolled = [pltpu.roll(col, step, 1) for col in cols]
-        lane = iota(cols[0].shape, 1)
-        return [jnp.where(lane >= step, one, two) for one, two in zip(rolled, [jnp.zeros_like(cols[0])] + rolled[:-1])]
+        lane = lane16 if cols[0].dtype == BF16 else lane8
+        return [jnp.where(lane >= jnp.asarray(step, lane.dtype), one, two) for one, two in zip(rolled, [jnp.zeros_like(cols[0])] + rolled[:-1])]
 
     def place_tables():
         dense = []
@@ -204,8 +208,8 @@
             for e in range(n_fft):
                 leaves, comes = (moves[e] >> k) & 1, (next_moves[e] >> k) & 1
                 at = slice(e * W, (e + 1) * W)
-                leave[k, :, at] = leaves
-                come[k, :, at] = comes
+                leave[k, :, at] = both(leaves.astype(F32)).astype(BF16)
+                come[k, :, at] = both(comes.astype(F32)).astype(BF16)
                 moves[e] = jnp.where(comes > 0, next_moves[e], jnp.where(leaves > 0, 0, moves[e]))
                 cols[e] = jnp.where(comes > 0, next_cols[e], jnp.where(leaves > 0, -1, cols[e]))
         for r in range(cap // W):
@@ -256,15 +260,13 @@
     def to_planes(b):
         wait_bytes(recv1.at[b, pl.ds(0, n_fft - 1)], r1.at[b])
 
-    def both(mask):
-        return jnp.concatenate([mask, mask], axis=0)
-
     def pack_sticks(b):
-        cols = [recv1[b, e].astype(F32) for e in range(n_fft)]
+        cols = [recv1[b, e] for e in range(n_fft)]
+        none = jnp.asarray(0, BF16)
         for k in range(bits):
             arriving = moved_left(cols, k)
-            cols = [jnp.where(both(come[k, :, e * W:(e + 1) * W]) > 0, arriving[e], cols[e]) for e in range(n_fft)]
-        dense[...] = jnp.concatenate(cols[:cap // W], axis=1).astype(BF16)
+            cols = [jnp.where(come[k, :, e * W:(e + 1) * W] > none, arriving[e], cols[e]) for e in range(n_fft)]
+        dense[...] = jnp.concatenate(cols[:cap // W], axis=1)
 
     def place_columns(b):
         sticks, place = dense[...], chi_b[...]
@@ -313,13 +315,14 @@
         found = jnp.zeros((nq, cap), F32)
         for i in range(LOW):
             found = jnp.where(place == float(i), rows[i * nq:(i + 1) * nq], found)
-        cols = [found[:, r * W:(r + 1) * W] for r in range(cap // W)]
-        cols = cols + [jnp.zeros((nq, W), F32)] * (n_fft - len(cols))
+        none = jnp.asarray(0, BF16)
+        cols = [found[:, r * W:(r + 1) * W].astype(BF16) for r in range(cap // W)]
+        cols = cols + [jnp.zeros((nq, W), BF16)] * (n_fft - len(cols))
         for k in reversed(range(bits)):
             leaving = moved_right(cols, k)
-            cols = [jnp.where(both(leave[k, :, e * W:(e + 1) * W]) > 0, leaving[e], cols[e]) for e in range(n_fft)]
+            cols = [jnp.where(leave[k, :, e * W:(e + 1) * W] > none, leaving[e], cols[e]) for e in range(n_fft)]
         for e in range(n_fft):
-            send2[b, e] = cols[e].astype(BF16)
+            send2[b, e] = cols[e]
         if after is not None:
             after()
         recv2[b, f] = send2[b, f]
@@ -485,8 +488,8 @@
             pltpu.VMEM((nq, cap), BF16),
             pltpu.VMEM((2, LOW * nq, W), F32),
             pltpu.VMEM((LOW * nq, 2 * W), BF16),
-            pltpu.VMEM(((n_fft * W - 1).bit_length(), 8, n_fft * W), jnp.int32),
-            pltpu.VMEM(((n_fft * W - 1).bit_length(), 8, n_fft * W), jnp.int32),
+            pltpu.VMEM(((n_fft * W - 1).bit_length(), nq, n_fft * W), BF16),
+            pltpu.VMEM(((n_fft * W - 1).bit_length(), nq, n_fft * W), BF16),
             pltpu.VMEM((n_chip, 2, 2, SLOTS, W), BF16),
             pltpu.VMEM(beta.shape, BF16),
             pltpu.VMEM((32 * PAD, W), F32),

time: 36 us -> 36.3 us (level)
  no operation moved by 1% of the time
where the time goes in v6:
time: 36.3 us; the launch traced here: 36.2 us
  Pallas kernels  34.6 us (95%)
  local copies, waits for them, and re-layouts  1.59 us (4%)
    pallas_call x1, Pallas kernels, body(): pl.pallas_call(functools.partial(kernel, n_band, n_fft), out_shape=jax.Sh...  34.6 us
    unnamed x1, local copies, waits for them, and re-layouts  1.59 us

profile of v6, /device:TPU:16, one launch (start us, length us, event | category | flops | bytes accessed | tf_op | source)
XLA Modules:
  0.0 36.2 jit_solution(4896006580999767597)
XLA Ops:
  0.0 34.6 %shard_map.118 = f32[2,2,80,128]{3,2,1,0:T(8,128)} custom-call(s32[2560]{0:T(1024)} %len_h.1, s32[2560]{0:T(1024)} %col_h.1, s32[1,256]{1,0:T(1,128)} %bitcast.5, s32[20,128]{1,0:T(8,128)} %bitcast.4, s32[20,128]{1,0:T(8,128)} %bitcast.3, bf16[2,2,80,128]{3,2,1,0:T(8,128)(2,1)} %psi_h.1, f32[8,57600]{1,0:T(8,128)} %pot_h.1, ...), custom_call_target="tpu_custom_call" | custom-call | tf_op jit(solution)/shard_map/pallas_call | solution.py:468
  34.6 1.6 %copy.14 = f32[2,2,80,128]{3,2,1,0:T(8,128)} copy(f32[2,2,80,128]{3,2,1,0:T(8,128)} %shard_map.118) | data formatting | bytes 327680

commit v7 on v5

--- a/solution.py
+++ b/solution.py
@@ -91,6 +91,8 @@
     chip = lax.div(g, 2)
     other = g + 1 - 2 * lax.rem(g, 2)
 
+    by_distance = sorted(range(1, n_chip), key=lambda k: abs(k - n_chip // 2))
+
     def same_core(k):
         return lax.rem(g + 2 * k, n_band)
 
@@ -152,7 +154,7 @@
             device_id={"band": same_core(k)}, device_id_type=MESH,
         )
 
-    for k in range(1, n_chip):
+    for k in by_distance:
         to_chips(k, psi_ref, gath.at[chip], sg, rg).start()
     loads[8].wait()
     swap_beta = pltpu.make_async_remote_copy(
@@ -373,7 +375,7 @@
                 term_f[pl.ds(m * 16 + i, nbr, stride=PAD), :] = terms[:, i * W:(i + 1) * W]
 
     def send_terms():
-        for k in reversed(range(n_chip)):
+        for k in by_distance + [0]:
             h = lax.div(same_core(k), 2)
             for i in range(4):
                 at = pl.ds(pl.multiple_of((h * 4 + i) * PAD, 8), SLOTS)

time: 36 us -> 36.3 us (level)
  no operation moved by 1% of the time
where the time goes in v7:
time: 36.3 us; the launch traced here: 35.9 us
  Pallas kernels  34.3 us (94%)
  local copies, waits for them, and re-layouts  1.59 us (4%)
    pallas_call x1, Pallas kernels, body(): pl.pallas_call(functools.partial(kernel, n_band, n_fft), out_shape=jax.Sh...  34.3 us
    unnamed x1, local copies, waits for them, and re-layouts  1.59 us

profile of v7, /device:TPU:16, one launch (start us, length us, event | category | flops | bytes accessed | tf_op | source)
XLA Modules:
  0.0 35.9 jit_solution(17112054453729227621)
XLA Ops:
  0.0 34.3 %shard_map.118 = f32[2,2,80,128]{3,2,1,0:T(8,128)} custom-call(s32[2560]{0:T(1024)} %len_h.1, s32[2560]{0:T(1024)} %col_h.1, s32[1,256]{1,0:T(1,128)} %bitcast.5, s32[20,128]{1,0:T(8,128)} %bitcast.4, s32[20,128]{1,0:T(8,128)} %bitcast.3, bf16[2,2,80,128]{3,2,1,0:T(8,128)(2,1)} %psi_h.1, f32[8,57600]{1,0:T(8,128)} %pot_h.1, ...), custom_call_target="tpu_custom_call" | custom-call | tf_op jit(solution)/shard_map/pallas_call | solution.py:467
  34.3 1.6 %copy.14 = f32[2,2,80,128]{3,2,1,0:T(8,128)} copy(f32[2,2,80,128]{3,2,1,0:T(8,128)} %shard_map.118) | data formatting | bytes 327680
